TPU v7x, 32 devices: a whole 2x2x4 slice. The times are simulated.
32 devices in a mesh: queue: 8 (over z, y), head: 4 (over x, core).
Axes of the slice: x: 2, y: 2, z: 4, core: 2. Of those that a mesh axis runs over, the one named last changes fastest.
Arguments:
- latents: bfloat16 [1536, 1536], P('queue', 'head'), may hold values from -6 to 6
- fresh_frame: bfloat16 [384, 1536], P(None, 'head'), may hold values from -6 to 6
- noise_level: int32 [4], replicated, may hold values from 0 to 15, as said below
- offset: int32 [1], replicated, may hold values from 0 to 16383
- mod_table: float32 [16, 3, 1536], replicated, may hold values from -4 to 4
- w_qkv: bfloat16 [1536, 3, 1536], P(None, None, 'head'), may hold values from -1 to 1
- w_out: bfloat16 [1536, 1536], P('head'), may hold values from -0.15625 to 0.15625
- q_gain: float32 [1536], P('head'), may hold values from 1 to 3
- k_gain: float32 [1536], P('head'), may hold values from 1 to 3
Outputs:
- advanced: bfloat16 [1536, 1536], P('queue', 'head')
Inputs may be any that keep to these rules, and one draw needn't show every extreme that they name: `noise_level`: entry p lies in p * 4 to (p + 1) * 4 - 1.
All inputs are finite; a program needn't handle non-finite values.
Results may differ from a plain program's by a relative error of at most 0.011.
Values may be sent and summed in bfloat16 or wider, within the bound.
A program may use at most 128 MiB of HBM per device.

v0:
```python
import jax
import jax.numpy as jnp
from jax import lax
from jax.sharding import PartitionSpec as P

D = 1536
DH = 128


def passed_along(block, axis, distance):
    devices = range(lax.axis_size(axis))
    route = [((i - distance) % len(devices), i) for i in devices]
    return lax.ppermute(block, axis, route)


def attend(carried, queries, key_block, value_block, allowed):
    run_max, run_total, running = carried
    key_count = key_block.shape[0]
    head_count = queries.shape[1]
    key_heads = key_block.reshape(key_count, head_count, DH)
    value_heads = value_block.reshape(key_count, head_count, DH)
    scores = jnp.einsum(
        "qhd,khd->hqk", queries, key_heads, preferred_element_type=jnp.float32
    ) * DH ** (-0.5)
    scores = jnp.where(allowed[None, None, :], scores, -jnp.inf)
    new_max = jnp.maximum(run_max, jnp.max(scores, axis=2))
    rescale = jnp.exp(run_max - new_max)
    exp_scores = jnp.exp(scores - new_max[:, :, None])
    new_total = run_total * rescale + jnp.sum(exp_scores, axis=2)
    added = jnp.einsum(
        "hqk,khd->hqd",
        exp_scores.astype(jnp.bfloat16),
        value_heads,
        preferred_element_type=jnp.float32,
    )
    return (new_max, new_total, running * rescale[:, :, None] + added)


def local(latents, fresh_frame, noise_level, offset, mod_table, w_qkv, w_out, q_gain, k_gain):
    slabs = lax.axis_size("queue")
    frames = slabs // 2
    my_slab = lax.axis_index("queue")
    my_frame = my_slab // 2
    position = jnp.mod(my_frame - offset[0], frames)
    my_level = noise_level[position]
    modulation = lax.dynamic_index_in_dim(mod_table, my_level, 0, keepdims=False)
    whole = lax.all_gather(latents, "head", axis=1, tiled=True).astype(jnp.float32)
    row_count = whole.shape[0]
    centered = whole - jnp.mean(whole, axis=1, keepdims=True)
    variance = jnp.mean(centered * centered, axis=1, keepdims=True)
    normed = centered * lax.rsqrt(variance + 1e-06)
    modded = (normed * (1.0 + modulation[1]) + modulation[0]).astype(jnp.bfloat16)
    local_width = w_qkv.shape[2]
    projected = jnp.dot(
        modded, w_qkv.reshape(w_qkv.shape[0], 3 * local_width), preferred_element_type=jnp.float32
    )
    projected = projected.reshape(row_count, 3, local_width)
    query_raw = projected[:, 0]
    key_raw = projected[:, 1]
    values = projected[:, 2].astype(jnp.bfloat16)
    query_sq, key_sq = lax.psum(
        (jnp.sum(query_raw * query_raw, axis=1), jnp.sum(key_raw * key_raw, axis=1)), "head"
    )
    queries = (query_raw * lax.rsqrt(query_sq / D + 1e-06)[:, None] * q_gain).astype(jnp.bfloat16)
    key_normed = (key_raw * lax.rsqrt(key_sq / D + 1e-06)[:, None] * k_gain).astype(jnp.bfloat16)
    head_count = local_width // DH
    query_heads = queries.reshape(row_count, head_count, DH)
    start_state = (
        jnp.full((head_count, row_count), -1e30, jnp.float32),
        jnp.zeros((head_count, row_count), jnp.float32),
        jnp.zeros((head_count, row_count, DH), jnp.float32),
    )
    all_rows = jnp.ones((row_count,), dtype=bool)
    carried = attend(start_state, query_heads, key_normed, values, all_rows)
    stacked = jnp.stack((key_normed, values))

    def pass_step(turn, loop_state):
        pieces, state_now = loop_state
        pieces = passed_along(pieces, "queue", 1)
        key_slab = jnp.mod(my_slab - turn, slabs)
        key_pos = jnp.mod(key_slab // 2 - offset[0], frames)

        def use_piece(state_in):
            return attend(state_in, query_heads, pieces[0], pieces[1], all_rows)

        def keep_state(state_in):
            return state_in

        state_now = lax.cond(key_pos <= position, use_piece, keep_state, state_now)
        return (pieces, state_now)

    stacked, carried = lax.fori_loop(1, slabs, pass_step, (stacked, carried))
    run_max, run_total, running = carried
    attn = (
        jnp.transpose(running / run_total[:, :, None], (1, 0, 2))
        .reshape(row_count, local_width)
        .astype(jnp.bfloat16)
    )
    partial_out = jnp.dot(attn, w_out, preferred_element_type=jnp.float32)
    proj = lax.psum_scatter(
        partial_out.astype(jnp.bfloat16), "head", scatter_dimension=1, tiled=True
    ).astype(jnp.float32)
    feature_start = lax.axis_index("head") * local_width
    gate_local = lax.dynamic_slice_in_dim(modulation[2], feature_start, local_width)
    updated = (latents.astype(jnp.float32) + gate_local * proj).astype(jnp.bfloat16)
    moved = passed_along(updated, "queue", -2)
    entry_slot = jnp.mod(offset[0] - 1, frames)
    fresh_half = lax.dynamic_slice_in_dim(fresh_frame, my_slab % 2 * row_count, row_count, 0)
    return jnp.where(my_frame == entry_slot, fresh_half, moved)


def solution(mesh):
    return jax.shard_map(
        local,
        mesh=mesh,
        in_specs=(
            P("queue", "head"),
            P(None, "head"),
            P(),
            P(),
            P(),
            P(None, None, "head"),
            P("head", None),
            P("head"),
            P("head"),
        ),
        out_specs=P("queue", "head"),
        check_vma=False,
    )
```

profile of v0, /device:TPU:0, one launch (start us, length us, event | category | flops | bytes accessed | tf_op | source)
XLA Modules:
  0.0 152.7 jit_solution(14749981668233794753)
XLA Ops:
  7.3 1.2 dynamic_slice.14
  9.9 9.2 %all_gather.3 = bf16[192,1536]{1,0:T(8,128)(2,1)S(1)} all-gather(bf16[192,384]{1,0:T(8,128)(2,1)} %param.13), channel_id=1, replica_groups=mesh['queue'=8,'head'=4] {'head'}, dimensions={1}, use_global_device_ids=true | all-gather | bytes 737280 | tf_op jit(solution)/shard_map/all_gather | solution.py:47
  19.0 0.2 convert_reduce_fusion
  19.2 0.3 fusion.10
  19.5 6.1 %copy.28 = bf16[1536,3,384]{0,2,1:T(8,128)(2,1)} copy(bf16[1536,3,384]{2,0,1:T(8,128)(2,1)} %param.18) | data formatting | bytes 7077888 | tf_op args[5]
  26.3 0.9 fusion.31
  27.1 3.3 %fusion.6 = f32[192,3,384]{2,0,1:T(8,128)S(1)} fusion(bf16[1536,3,384]{0,2,1:T(8,128)(2,1)} %copy.28, bf16[192,1536]{1,0:T(8,128)(2,1)S(1)} %all_gather.3, f32[1536]{0:T(1024)S(1)} %get-tuple-element.327, f32[1536]{0:T(1024)S(1)} %get-tuple-element.326, f32[192]{0:T(256)S(1)} %add_rsqrt_fusion.2, f32[192]{0:T(256)S(1)} %broadcast_multiply_fusion), kind=kOutput, calls=%fused_computation.10 | convolution fusion | flops 681246720 | bytes 5027328 | tf_op jit(solution)/shard_map/dot_general | solution.py:54
  30.4 0.2 multiply_reduce_fusion
  30.6 0.7 slice.40
  31.3 0.1 squeeze.41
  31.5 0.1 squeeze.40
  31.6 6.7 %all-reduce = (f32[192]{0:T(256)S(1)}, f32[192]{0:T(256)S(1)}) all-reduce(f32[192]{0:T(256)S(1)} %get-tuple-element.325, f32[192]{0:T(256)S(1)} %get-tuple-element.324), channel_id=1, replica_groups=mesh['queue'=8,'head'=4] {'head'}, use_global_device_ids=true, to_apply=%region_3.4 | all-reduce | flops 384 | bytes 3072 | tf_op jit(solution)/shard_map/psum | solution.py:61
  38.3 0.3 multiply_convert_fusion.1
  38.6 0.1 fusion.24
  38.7 0.3 multiply_convert_fusion
  39.0 0.3 fusion.35
  39.3 0.1 fusion.21
  39.4 0.1 copy-done.2
  39.6 0.3 convolution_add_fusion.1
  40.0 75.6 %while.22 = (s32[]{:T(128)}, bf16[2,192,384]{2,1,0:T(8,128)(2,1)S(1)}, f32[3,192]{1,0:T(4,128)S(1)}, f32[3,192]{1,0:T(4,128)S(1)}, f32[3,192,128]{2,1,0:T(8,128)...) while((s32[]{:T(128)}, ...), condition=%wide.region_13.14_spmd, body=%wide.region_8.13_spmd.sunk | while | flops 57435304 | bytes 5345971 | solution.py:92
  40.0 1.6 %collective-permute-start = (bf16[2,192,384]{2,1,0:T(8,128)(2,1)S(1)}, bf16[2,192,384]{2,1,0:T(8,128)(2,1)S(1)}, u32[]{:S(2)}, u32[]{:S(2)}) collective-permute-start(bf16[2,192,384]{2,1,0:T(8,128)(2,1)S(1)} %get-tuple-element.446), channel_id=1, source_target_pairs={{28,0},{0,4},{4,8},{8,12},{12,16},{16,20},{20,24},{24,28},{29,1},{... | collective-permute-start | bytes 884744 | tf_op jit(solution)/shard_map/while/body/eval_jaxpr/ppermute | solution.py:13
  42.2 8.4 %collective-permute-done = bf16[2,192,384]{2,1,0:T(8,128)(2,1)S(1)} collective-permute-done((bf16[2,192,384]{2,1,0:T(8,128)(2,1)S(1)}, bf16[2,192,384]{2,1,0:T(8,128)(2,1)S(1)}, u32[]{:S(2)}, u32[]{:S(2)}) %collective-permute-start) | collective-permute-done | bytes 294944 | tf_op jit(solution)/shard_map/while/body/eval_jaxpr/ppermute | solution.py:13
  50.6 0.9 conditional.2
  50.7 0.3 fusion.34
  51.0 0.1 fusion.1
  51.2 0.4 convolution_add_fusion
  51.6 0.1 collective-permute-start
  52.4 8.9 %collective-permute-done = bf16[2,192,384]{2,1,0:T(8,128)(2,1)S(1)} collective-permute-done((bf16[2,192,384]{2,1,0:T(8,128)(2,1)S(1)}, bf16[2,192,384]{2,1,0:T(8,128)(2,1)S(1)}, u32[]{:S(2)}, u32[]{:S(2)}) %collective-permute-start) | collective-permute-done | bytes 294944 | tf_op jit(solution)/shard_map/while/body/eval_jaxpr/ppermute | solution.py:13
  61.3 0.9 conditional.2
  61.4 0.3 fusion.34
  61.7 0.1 fusion.1
  61.9 0.4 convolution_add_fusion
  62.3 0.1 collective-permute-start
  63.1 8.7 %collective-permute-done = bf16[2,192,384]{2,1,0:T(8,128)(2,1)S(1)} collective-permute-done((bf16[2,192,384]{2,1,0:T(8,128)(2,1)S(1)}, bf16[2,192,384]{2,1,0:T(8,128)(2,1)S(1)}, u32[]{:S(2)}, u32[]{:S(2)}) %collective-permute-start) | collective-permute-done | bytes 294944 | tf_op jit(solution)/shard_map/while/body/eval_jaxpr/ppermute | solution.py:13
  71.8 0.9 conditional.2
  71.9 0.3 fusion.34
  72.1 0.1 fusion.1
  72.3 0.4 convolution_add_fusion
  72.8 0.1 collective-permute-start
  73.5 8.7 %collective-permute-done = bf16[2,192,384]{2,1,0:T(8,128)(2,1)S(1)} collective-permute-done((bf16[2,192,384]{2,1,0:T(8,128)(2,1)S(1)}, bf16[2,192,384]{2,1,0:T(8,128)(2,1)S(1)}, u32[]{:S(2)}, u32[]{:S(2)}) %collective-permute-start) | collective-permute-done | bytes 294944 | tf_op jit(solution)/shard_map/while/body/eval_jaxpr/ppermute | solution.py:13
  82.2 0.9 conditional.2
  82.3 0.3 fusion.34
  82.6 0.1 fusion.1
  82.8 0.4 convolution_add_fusion
  83.2 0.1 collective-permute-start
  84.0 9.6 %collective-permute-done = bf16[2,192,384]{2,1,0:T(8,128)(2,1)S(1)} collective-permute-done((bf16[2,192,384]{2,1,0:T(8,128)(2,1)S(1)}, bf16[2,192,384]{2,1,0:T(8,128)(2,1)S(1)}, u32[]{:S(2)}, u32[]{:S(2)}) %collective-permute-start) | collective-permute-done | bytes 294944 | tf_op jit(solution)/shard_map/while/body/eval_jaxpr/ppermute | solution.py:13
  93.6 0.1 collective-permute-start
  94.4 10.7 %collective-permute-done = bf16[2,192,384]{2,1,0:T(8,128)(2,1)S(1)} collective-permute-done((bf16[2,192,384]{2,1,0:T(8,128)(2,1)S(1)}, bf16[2,192,384]{2,1,0:T(8,128)(2,1)S(1)}, u32[]{:S(2)}, u32[]{:S(2)}) %collective-permute-start) | collective-permute-done | bytes 294944 | tf_op jit(solution)/shard_map/while/body/eval_jaxpr/ppermute | solution.py:13
  105.2 0.1 collective-permute-start
  105.9 8.7 %collective-permute-done = bf16[2,192,384]{2,1,0:T(8,128)(2,1)S(1)} collective-permute-done((bf16[2,192,384]{2,1,0:T(8,128)(2,1)S(1)}, bf16[2,192,384]{2,1,0:T(8,128)(2,1)S(1)}, u32[]{:S(2)}, u32[]{:S(2)}) %collective-permute-start) | collective-permute-done | bytes 294944 | tf_op jit(solution)/shard_map/while/body/eval_jaxpr/ppermute | solution.py:13
  114.6 0.9 conditional.2
  114.7 0.3 fusion.34
  115.0 0.1 fusion.1
  115.2 0.4 convolution_add_fusion
  115.6 0.5 convolution_convert_fusion
  116.2 1.2 copy.37
  117.4 0.0 reduce-scatter.4.cloned.1.call-update
  117.4 0.8 dynamic-slice_reduce_fusion.1
  118.2 19.3 %reduce-scatter.4.cloned.1.call-done = bf16[384,192]{1,0:T(8,128)(2,1)} async-done(((bf16[1536,192]{1,0:T(8,128)(2,1)}), bf16[384,192]{1,0:T(8,128)(2,1)}) %reduce-scatter.4.cloned.1.call-update) | async-done | bytes 147472
  137.5 1.1 copy.38
  138.6 0.1 add_convert_fusion
  138.6 3.4 %collective-permute-start.1 = (bf16[192,384]{1,0:T(8,128)(2,1)S(1)}, bf16[192,384]{1,0:T(8,128)(2,1)S(1)}, u32[]{:S(2)}, u32[]{:S(2)}) collective-permute-start(bf16[192,384]{1,0:T(8,128)(2,1)S(1)} %add_convert_fusion), channel_id=1, source_target_pairs={{8,0},{12,4},{16,8},{20,12},{24,16},{28,20},{0,24},{4,28},{9,1},{1... | collective-permute-start | bytes 442376 | tf_op jit(solution)/shard_map/ppermute | solution.py:13
  142.0 3.1 %collective-permute-done.1 = bf16[192,384]{1,0:T(8,128)(2,1)S(1)} collective-permute-done((bf16[192,384]{1,0:T(8,128)(2,1)S(1)}, bf16[192,384]{1,0:T(8,128)(2,1)S(1)}, u32[]{:S(2)}, u32[]{:S(2)}) %collective-permute-start.1) | collective-permute-done | bytes 147488 | tf_op jit(solution)/shard_map/ppermute | solution.py:13
  145.1 0.7 dynamic-slice_select_fusion
  (60 shorter events, 1.2 us)
Async XLA Ops:
  6.5 109.1 %copy-start = (bf16[384,1536]{1,0:T(8,128)(2,1)S(1)}, bf16[384,1536]{1,0:T(8,128)(2,1)}, u32[]{:S(2)}) copy-start(bf16[384,1536]{1,0:T(8,128)(2,1)} %param.19) | copy-start | bytes 3538948
  6.5 131.0 %reduce-scatter.4.cloned.1.call-start = ((), (), s32[]{:S(2)}) async-start(), calls=%async_computation.1 | async-start | bytes 983040
  30.6 7.7 %copy-start.5 = (f32[384]{0:T(512)S(1)}, f32[384]{0:T(512)}, u32[]{:S(2)}) copy-start(f32[384]{0:T(512)} %param.20) | copy-start | bytes 4612
  31.3 7.3 %copy-start.4 = (f32[384]{0:T(512)S(1)}, f32[384]{0:T(512)}, u32[]{:S(2)}) copy-start(f32[384]{0:T(512)} %param.21) | copy-start | bytes 4612
  38.6 0.9 copy-start.2
  40.0 10.6 %collective-permute-start = (bf16[2,192,384]{2,1,0:T(8,128)(2,1)S(1)}, bf16[2,192,384]{2,1,0:T(8,128)(2,1)S(1)}, u32[]{:S(2)}, u32[]{:S(2)}) collective-permute-start(bf16[2,192,384]{2,1,0:T(8,128)(2,1)S(1)} %get-tuple-element.446), channel_id=1, source_target_pairs={{28,0},{0,4},{4,8},{8,12},{12,16},{16,20},{20,24},{24,28},{29,1},{... | collective-permute-start | bytes 884744 | tf_op jit(solution)/shard_map/while/body/eval_jaxpr/ppermute | solution.py:13
  51.6 9.7 %collective-permute-start = (bf16[2,192,384]{2,1,0:T(8,128)(2,1)S(1)}, bf16[2,192,384]{2,1,0:T(8,128)(2,1)S(1)}, u32[]{:S(2)}, u32[]{:S(2)}) collective-permute-start(bf16[2,192,384]{2,1,0:T(8,128)(2,1)S(1)} %get-tuple-element.446), channel_id=1, source_target_pairs={{28,0},{0,4},{4,8},{8,12},{12,16},{16,20},{20,24},{24,28},{29,1},{... | collective-permute-start | bytes 884744 | tf_op jit(solution)/shard_map/while/body/eval_jaxpr/ppermute | solution.py:13
  62.3 9.5 %collective-permute-start = (bf16[2,192,384]{2,1,0:T(8,128)(2,1)S(1)}, bf16[2,192,384]{2,1,0:T(8,128)(2,1)S(1)}, u32[]{:S(2)}, u32[]{:S(2)}) collective-permute-start(bf16[2,192,384]{2,1,0:T(8,128)(2,1)S(1)} %get-tuple-element.446), channel_id=1, source_target_pairs={{28,0},{0,4},{4,8},{8,12},{12,16},{16,20},{20,24},{24,28},{29,1},{... | collective-permute-start | bytes 884744 | tf_op jit(solution)/shard_map/while/body/eval_jaxpr/ppermute | solution.py:13
  72.8 9.5 %collective-permute-start = (bf16[2,192,384]{2,1,0:T(8,128)(2,1)S(1)}, bf16[2,192,384]{2,1,0:T(8,128)(2,1)S(1)}, u32[]{:S(2)}, u32[]{:S(2)}) collective-permute-start(bf16[2,192,384]{2,1,0:T(8,128)(2,1)S(1)} %get-tuple-element.446), channel_id=1, source_target_pairs={{28,0},{0,4},{4,8},{8,12},{12,16},{16,20},{20,24},{24,28},{29,1},{... | collective-permute-start | bytes 884744 | tf_op jit(solution)/shard_map/while/body/eval_jaxpr/ppermute | solution.py:13
  83.2 10.3 %collective-permute-start = (bf16[2,192,384]{2,1,0:T(8,128)(2,1)S(1)}, bf16[2,192,384]{2,1,0:T(8,128)(2,1)S(1)}, u32[]{:S(2)}, u32[]{:S(2)}) collective-permute-start(bf16[2,192,384]{2,1,0:T(8,128)(2,1)S(1)} %get-tuple-element.446), channel_id=1, source_target_pairs={{28,0},{0,4},{4,8},{8,12},{12,16},{16,20},{20,24},{24,28},{29,1},{... | collective-permute-start | bytes 884744 | tf_op jit(solution)/shard_map/while/body/eval_jaxpr/ppermute | solution.py:13
  93.6 11.5 %collective-permute-start = (bf16[2,192,384]{2,1,0:T(8,128)(2,1)S(1)}, bf16[2,192,384]{2,1,0:T(8,128)(2,1)S(1)}, u32[]{:S(2)}, u32[]{:S(2)}) collective-permute-start(bf16[2,192,384]{2,1,0:T(8,128)(2,1)S(1)} %get-tuple-element.446), channel_id=1, source_target_pairs={{28,0},{0,4},{4,8},{8,12},{12,16},{16,20},{20,24},{24,28},{29,1},{... | collective-permute-start | bytes 884744 | tf_op jit(solution)/shard_map/while/body/eval_jaxpr/ppermute | solution.py:13
  105.2 9.5 %collective-permute-start = (bf16[2,192,384]{2,1,0:T(8,128)(2,1)S(1)}, bf16[2,192,384]{2,1,0:T(8,128)(2,1)S(1)}, u32[]{:S(2)}, u32[]{:S(2)}) collective-permute-start(bf16[2,192,384]{2,1,0:T(8,128)(2,1)S(1)} %get-tuple-element.446), channel_id=1, source_target_pairs={{28,0},{0,4},{4,8},{8,12},{12,16},{16,20},{20,24},{24,28},{29,1},{... | collective-permute-start | bytes 884744 | tf_op jit(solution)/shard_map/while/body/eval_jaxpr/ppermute | solution.py:13
  116.2 22.4 %copy-start.1 = (bf16[192,384]{1,0:T(8,128)(2,1)S(1)}, bf16[192,384]{1,0:T(8,128)(2,1)}, u32[]{:S(2)}) copy-start(bf16[192,384]{1,0:T(8,128)(2,1)} %param.13) | copy-start | bytes 442372
  116.2 28.9 %copy-start.3 = (bf16[384,384]{1,0:T(8,128)(2,1)S(1)}, bf16[384,384]{1,0:T(8,128)(2,1)}, u32[]{:S(2)}) copy-start(bf16[384,384]{1,0:T(8,128)(2,1)} %param.14) | copy-start | bytes 884740
  138.6 6.5 %collective-permute-start.1 = (bf16[192,384]{1,0:T(8,128)(2,1)S(1)}, bf16[192,384]{1,0:T(8,128)(2,1)S(1)}, u32[]{:S(2)}, u32[]{:S(2)}) collective-permute-start(bf16[192,384]{1,0:T(8,128)(2,1)S(1)} %add_convert_fusion), channel_id=1, source_target_pairs={{8,0},{12,4},{16,8},{20,12},{24,16},{28,20},{0,24},{4,28},{9,1},{1... | collective-permute-start | bytes 442376 | tf_op jit(solution)/shard_map/ppermute | solution.py:13
Sparse Core Ops, SparseCore 0:
  117.5 19.9 reduce-scatter.3
where the time goes:
time: 153 us
  waiting for transfers between devices  86.1 us (56%)
  between operations  16.3 us (11%)
  blocking collectives  15.9 us (10%)
  local copies, waits for them, and re-layouts  12.3 us (8%)
  matrix products  7.69 us (5%)
  loops' own time  5.33 us (3%)
  starting transfers between devices  5.28 us (3%)
  other arithmetic  3.73 us (2%)
    ppermute x8, waiting for transfers between devices, passed_along(): return lax.ppermute(block, axis, route)  66.8 us
    unnamed x2, waiting for transfers between devices  19.3 us
    all_gather x1, blocking collectives, local(): lax.all_gather(latents, 'head', axis=1, tiled=True).astype(jnp.float32)  9.19 us
    unnamed x15, local copies, waits for them, and re-layouts  8.42 us
    psum x1, blocking collectives, local(): lax.psum((jnp.sum(query_raw * query_raw, axis=1), jnp.sum(key_raw * key_r...  6.72 us
    ppermute x8, starting transfers between devices, passed_along(): return lax.ppermute(block, axis, route)  5.28 us
    another operation x1, loops' own time, local(): stacked, carried = lax.fori_loop(1, slabs, pass_step, (stacked, carried))  5.16 us
    dot_general x1, matrix products, local(): jnp.dot(modded, w_qkv.reshape(w_qkv.shape[0], 3 * local_width), preferred...  3.31 us
  transfers between devices with their start and end apart: 9, of which 9 were waited for; matrix products, arithmetic and copies ran while one was open for 1% of the time, Pallas kernels for 0%

commit v1 on v0

--- a/solution.py
+++ b/solution.py
@@ -1,6 +1,8 @@
 import jax
 import jax.numpy as jnp
 from jax import lax
+from jax.experimental import pallas as pl
+from jax.experimental.pallas import tpu as pltpu
 from jax.sharding import PartitionSpec as P
 
 D = 1536
@@ -109,9 +111,312 @@
     return jnp.where(my_frame == entry_slot, fresh_half, moved)
 
 
+MESH = pl.DeviceIdType.MESH
+ZS = 4
+ROWS = 192
+WIDTH = 384
+HEADS_DEV = 3
+
+
+def arrived(buffer, sem):
+    pltpu.make_async_copy(buffer, buffer, sem).wait()
+
+
+def block_kernel(
+    noise_ref, offset_ref, lat_ref, gain_ref, w_hbm, wout_hbm, mod_hbm, out_ref,
+    w_v, wo_v, mod_v, lat_buf, mod_act, raw, stat_buf, stage, q_buf, k_buf, v_buf,
+    o_buf, a_buf, p_send, rs_buf, upd, fin,
+    load_sem, lat_send, lat_recv, st_send, st_recv, qkv_send, q_recv, k_recv, v_recv,
+    f_send, o_send, o_recv, rs_send, rs_recv, mv_send, mv_recv,
+):
+    queue = lax.axis_index("queue")
+    head = lax.axis_index("head")
+    z, y = queue // 2, queue % 2
+    x, c = head // 2, head % 2
+    sib = x * 2 + (1 - c)
+    xnb = (1 - x) * 2 + c
+    diag = (1 - x) * 2 + (1 - c)
+    peers = (head, sib, xnb, diag)
+    below = queue - 2 + jnp.where(z == 0, 2 * ZS, 0)
+    above = queue + 2 - jnp.where(z == ZS - 1, 2 * ZS, 0)
+    swap_head = x * 2 + y
+    on_diagonal = y == c
+
+    def is_self(zt):
+        return jnp.logical_and(on_diagonal, zt == z)
+
+    loads = [
+        pltpu.make_async_copy(mod_hbm, mod_v, load_sem.at[0]),
+        pltpu.make_async_copy(w_hbm, w_v, load_sem.at[1]),
+        pltpu.make_async_copy(wout_hbm, wo_v, load_sem.at[2]),
+    ]
+    for load in loads:
+        load.start()
+
+    barrier = pltpu.get_barrier_semaphore()
+
+    def greet(q_id, h_id):
+        pl.semaphore_signal(barrier, inc=1, device_id=(q_id, h_id), device_id_type=MESH)
+
+    for peer in peers[1:]:
+        greet(queue, peer)
+    greet(below, head)
+    greet(above, head)
+    for zt in range(ZS):
+        pl.when(jnp.logical_not(is_self(zt)))(lambda zt=zt: greet(zt * 2 + c, swap_head))
+    pl.semaphore_wait(barrier, 5 + ZS - jnp.where(on_diagonal, 1, 0))
+
+    def remote(src, dst, s_sem, r_sem, q_id, h_id):
+        return pltpu.make_async_remote_copy(
+            src_ref=src, dst_ref=dst, send_sem=s_sem, recv_sem=r_sem,
+            device_id=(q_id, h_id), device_id_type=MESH,
+        )
+
+    to_x = remote(lat_ref, lat_buf.at[2], lat_send.at[0], lat_recv.at[2], queue, xnb)
+    to_sib = remote(lat_ref, lat_buf.at[1], lat_send.at[1], lat_recv.at[1], queue, sib)
+    to_x.start()
+    to_sib.start()
+    forward = remote(lat_buf.at[2], lat_buf.at[3], lat_send.at[2], lat_recv.at[3], queue, sib)
+    arrived(lat_buf.at[2], lat_recv.at[2])
+    forward.start()
+    arrived(lat_buf.at[1], lat_recv.at[1])
+    loads[0].wait()
+
+    offset = lax.rem(offset_ref[0], ZS)
+
+    def position_of(frame):
+        return lax.rem(frame + ZS - offset, ZS)
+
+    level = noise_ref[position_of(z)]
+    arrived(lat_buf.at[3], lat_recv.at[3])
+
+    def block(r):
+        return (lat_ref[...] if r == 0 else lat_buf[r]).astype(jnp.float32)
+
+    def columns(r):
+        return pl.ds(pl.multiple_of(peers[r] * WIDTH, WIDTH), WIDTH)
+
+    mean = sum(jnp.sum(block(r), axis=1, keepdims=True) for r in range(4)) / D
+    square = jnp.zeros((ROWS, 1), jnp.float32)
+    for r in range(4):
+        centered = block(r) - mean
+        square += jnp.sum(centered * centered, axis=1, keepdims=True)
+    inv = lax.rsqrt(square / D + 1e-06)
+    for r in range(4):
+        shift = mod_v[0, pl.ds(level, 1), columns(r)]
+        scale = mod_v[1, pl.ds(level, 1), columns(r)]
+        normed = (block(r) - mean) * inv
+        mod_act[:, columns(r)] = (normed * (1.0 + scale) + shift).astype(jnp.bfloat16)
+
+    loads[1].wait()
+    sums = []
+    for i in range(2):
+        projected = jnp.dot(mod_act[...], w_v[i], preferred_element_type=jnp.float32)
+        raw[i] = projected
+        sums.append(jnp.sum(projected * projected, axis=1, keepdims=True))
+    lane = lax.broadcasted_iota(jnp.int32, (256, 128), 1)
+    padding = jnp.zeros((256 - ROWS, 1), jnp.float32)
+    spread = jnp.where(
+        lane == 0,
+        jnp.concatenate([sums[0], padding], axis=0),
+        jnp.concatenate([sums[1], padding], axis=0),
+    )
+    stat_buf[0] = jnp.transpose(spread)[:8]
+    stats = [
+        remote(stat_buf.at[0], stat_buf.at[r], st_send.at[r], st_recv.at[r], queue, peers[r])
+        for r in (2, 3, 1)
+    ]
+    for copy in stats:
+        copy.start()
+
+    sends = []
+
+    def send_part(part, buf, recv_sem):
+        for j in range(HEADS_DEV):
+            zt = j + c
+            mine = is_self(zt)
+            src = stage.at[part, j]
+            dst = buf.at[z] if part == 0 else buf.at[0, z]
+            far = remote(src, dst, qkv_send.at[part, j], recv_sem.at[z], zt * 2 + c, swap_head)
+            near = pltpu.make_async_copy(src, dst, recv_sem.at[z])
+            pl.when(mine)(near.start)
+            pl.when(jnp.logical_not(mine))(far.start)
+            sends.append((mine, far))
+
+    values = jnp.dot(mod_act[...], w_v[2], preferred_element_type=jnp.float32)
+    for j in range(HEADS_DEV):
+        stage[2, j] = values[:, j * DH:(j + 1) * DH].astype(jnp.bfloat16)
+    send_part(2, v_buf, v_recv)
+
+    for r in (1, 2, 3):
+        arrived(stat_buf.at[r], st_recv.at[r])
+    total_sq = stat_buf[0] + stat_buf[1] + stat_buf[2] + stat_buf[3]
+    rates = lax.rsqrt(total_sq / D + 1e-06)
+    rates = jnp.transpose(jnp.concatenate([rates] * 16, axis=0))[:ROWS]
+    for part, buf, recv_sem in ((1, k_buf, k_recv), (0, q_buf, q_recv)):
+        rate = rates[:, part:part + 1]
+        for j in range(HEADS_DEV):
+            cols = slice(j * DH, (j + 1) * DH)
+            stage[part, j] = (raw[part, :, cols] * rate * gain_ref[part:part + 1, cols]).astype(jnp.bfloat16)
+        send_part(part, buf, recv_sem)
+
+    active = jnp.logical_and(z - y >= 0, z - y <= 2)
+    slot = jnp.where(active, z - y, 0)
+
+    @pl.when(active)
+    def _():
+        forwards = []
+        for kind, (buf, recv_sem) in enumerate(((v_buf, v_recv), (k_buf, k_recv))):
+            for s in range(ZS):
+                arrived(buf.at[0, s], recv_sem.at[s])
+                copy = remote(
+                    buf.at[0, s], buf.at[1, s], f_send.at[kind, s], recv_sem.at[ZS + s], queue, sib
+                )
+                copy.start()
+                forwards.append(copy)
+        for s in range(ZS):
+            arrived(q_buf.at[s], q_recv.at[s])
+        for buf, recv_sem in ((v_buf, v_recv), (k_buf, k_recv)):
+            for s in range(ZS):
+                arrived(buf.at[1, s], recv_sem.at[ZS + s])
+        keys = k_buf[...].reshape(2 * ZS * ROWS, DH)
+        vals = v_buf[...].reshape(2 * ZS * ROWS, DH)
+        column = lax.broadcasted_iota(jnp.int32, (1, 2 * ZS * ROWS), 1)
+        frame = jnp.zeros_like(column)
+        for t in range(1, 2 * ZS):
+            frame += jnp.where(column >= t * ROWS, 1 if t != ZS else 1 - ZS, 0)
+        key_pos = frame - offset
+        key_pos = jnp.where(key_pos < 0, key_pos + ZS, key_pos)
+        outs = []
+        for s in range(ZS):
+            bias = jnp.where(key_pos <= position_of(s), 0.0, -1e30)
+            scores = lax.dot_general(
+                q_buf[s], keys, (((1,), (1,)), ((), ())), preferred_element_type=jnp.float32
+            )
+            scores = scores * DH ** (-0.5) + bias
+            top = jnp.max(scores, axis=1, keepdims=True)
+            e = jnp.exp(scores - top)
+            total = jnp.sum(e, axis=1, keepdims=True)
+            added = jnp.dot(e.astype(jnp.bfloat16), vals, preferred_element_type=jnp.float32)
+            o_buf[s] = (added / total).astype(jnp.bfloat16)
+            mine = is_self(s)
+            far = remote(
+                o_buf.at[s], a_buf.at[slot], o_send.at[s], o_recv.at[slot], s * 2 + c, swap_head
+            )
+            near = pltpu.make_async_copy(o_buf.at[s], a_buf.at[slot], o_recv.at[slot])
+            pl.when(mine)(near.start)
+            pl.when(jnp.logical_not(mine))(far.start)
+            outs.append((mine, far))
+        for copy in forwards:
+            copy.wait_send()
+        for mine, far in outs:
+            pl.when(jnp.logical_not(mine))(far.wait_send)
+
+    loads[2].wait()
+    for j in range(HEADS_DEV):
+        arrived(a_buf.at[j], o_recv.at[j])
+    attn = jnp.concatenate([a_buf[j] for j in range(HEADS_DEV)], axis=1)
+
+    def out_block(r):
+        return jnp.dot(attn, wo_v[:, columns(r)], preferred_element_type=jnp.float32)
+
+    p_send[0] = out_block(3).astype(jnp.bfloat16)
+    send_a = remote(p_send.at[0], rs_buf.at[0], rs_send.at[0], rs_recv.at[0], queue, sib)
+    send_a.start()
+    ahead = out_block(2)
+    p_send[1] = out_block(1).astype(jnp.bfloat16)
+    send_b = remote(p_send.at[1], rs_buf.at[1], rs_send.at[1], rs_recv.at[1], queue, sib)
+    send_b.start()
+    arrived(rs_buf.at[0], rs_recv.at[0])
+    p_send[2] = (ahead + rs_buf[0].astype(jnp.float32)).astype(jnp.bfloat16)
+    send_c = remote(p_send.at[2], rs_buf.at[2], rs_send.at[2], rs_recv.at[2], queue, xnb)
+    send_c.start()
+    proj = out_block(0)
+    arrived(rs_buf.at[1], rs_recv.at[1])
+    proj += rs_buf[1].astype(jnp.float32)
+    gate = mod_v[2, pl.ds(level, 1), columns(0)]
+    arrived(rs_buf.at[2], rs_recv.at[2])
+    proj += rs_buf[2].astype(jnp.float32)
+    upd[...] = (lat_ref[...].astype(jnp.float32) + gate * proj).astype(jnp.bfloat16)
+    move = remote(upd, fin, mv_send, mv_recv, below, head)
+    move.start()
+    for copy in (to_x, to_sib, forward, *stats, send_a, send_b, send_c):
+        copy.wait_send()
+    for mine, far in sends:
+        pl.when(jnp.logical_not(mine))(far.wait_send)
+    move.wait_send()
+    arrived(fin, mv_recv)
+    out_ref[...] = fin[...]
+
+
+def local_fused(latents, fresh_frame, noise_level, offset, mod_table, w_qkv, w_out, q_gain, k_gain):
+    bf16, f32 = jnp.bfloat16, jnp.float32
+    dma = pltpu.SemaphoreType.DMA
+    smem = pl.BlockSpec(memory_space=pltpu.SMEM)
+    vmem = pl.BlockSpec(memory_space=pltpu.VMEM)
+    hbm = pl.BlockSpec(memory_space=pl.ANY)
+    moved = pl.pallas_call(
+        block_kernel,
+        out_shape=jax.ShapeDtypeStruct((ROWS, WIDTH), bf16),
+        in_specs=[smem, smem, vmem, vmem, hbm, hbm, hbm],
+        out_specs=vmem,
+        scratch_shapes=[
+            pltpu.VMEM((3, D, WIDTH), bf16),
+            pltpu.VMEM((WIDTH, D), bf16),
+            pltpu.VMEM((3, mod_table.shape[0], D), f32),
+            pltpu.VMEM((4, ROWS, WIDTH), bf16),
+            pltpu.VMEM((ROWS, D), bf16),
+            pltpu.VMEM((2, ROWS, WIDTH), f32),
+            pltpu.VMEM((4, 8, 256), f32),
+            pltpu.VMEM((3, HEADS_DEV, ROWS, DH), bf16),
+            pltpu.VMEM((ZS, ROWS, DH), bf16),
+            pltpu.VMEM((2, ZS, ROWS, DH), bf16),
+            pltpu.VMEM((2, ZS, ROWS, DH), bf16),
+            pltpu.VMEM((ZS, ROWS, DH), bf16),
+            pltpu.VMEM((HEADS_DEV, ROWS, DH), bf16),
+            pltpu.VMEM((3, ROWS, WIDTH), bf16),
+            pltpu.VMEM((3, ROWS, WIDTH), bf16),
+            pltpu.VMEM((ROWS, WIDTH), bf16),
+            pltpu.VMEM((ROWS, WIDTH), bf16),
+            dma((3,)),
+            dma((3,)),
+            dma((4,)),
+            dma((4,)),
+            dma((4,)),
+            dma((3, HEADS_DEV)),
+            dma((ZS,)),
+            dma((2 * ZS,)),
+            dma((2 * ZS,)),
+            dma((2, ZS)),
+            dma((ZS,)),
+            dma((HEADS_DEV,)),
+            dma((3,)),
+            dma((3,)),
+            dma,
+            dma,
+        ],
+        compiler_params=pltpu.CompilerParams(
+            collective_id=0, has_side_effects=True, vmem_limit_bytes=48 * 1024 * 1024
+        ),
+    )(
+        noise_level,
+        offset,
+        latents,
+        jnp.stack((q_gain, k_gain)),
+        jnp.transpose(w_qkv, (1, 0, 2)),
+        w_out,
+        jnp.transpose(mod_table, (1, 0, 2)),
+    )
+    my_slab = lax.axis_index("queue")
+    entry_slot = jnp.mod(offset[0] - 1, ZS)
+    fresh_half = lax.dynamic_slice_in_dim(fresh_frame, my_slab % 2 * ROWS, ROWS, 0)
+    return jnp.where(my_slab // 2 == entry_slot, fresh_half, moved)
+
+
 def solution(mesh):
+    fits = mesh.shape["queue"] == 2 * ZS and mesh.shape["head"] == 4
     return jax.shard_map(
-        local,
+        local_fused if fits else local,
         mesh=mesh,
         in_specs=(
             P("queue", "head"),

time: 153 us -> 54.3 us (0.35)
  waiting for transfers between devices: 86.1 us -> 0 us
  Pallas kernels: 0 us -> 45.4 us
  blocking collectives: 15.9 us -> 0 us
  between operations: 16.3 us -> 0.73 us
  matrix products: 7.69 us -> 0 us
  loops' own time: 5.33 us -> 0 us
  starting transfers between devices: 5.28 us -> 0 us
  local copies, waits for them, and re-layouts: 12.3 us -> 7.16 us
  other arithmetic: 3.73 us -> 0.71 us
    ppermute x8 -> x0, waiting for transfers between devices: 66.8 us -> none  [passed_along(): return lax.ppermute(block, axis, route)]
    pallas_call x0 -> x1, Pallas kernels: none -> 45.4 us  [local_fused(): pl.pallas_call(block_kernel, out_shape=jax.ShapeDtypeStruct((ROWS, WIDTH)...]
    unnamed x2 -> x0, waiting for transfers between devices: 19.3 us -> none
    all_gather x1 -> x0, blocking collectives: 9.19 us -> none  [local(): lax.all_gather(latents, 'head', axis=1, tiled=True).astype(jnp.float32)]
    dot_general x14 -> x0, matrix products: 7.69 us -> none  [the longest x1 3.31 us: local(): jnp.dot(modded, w_qkv.reshape(w_qkv.shape[0], 3 * local_width), preferred...]
    psum x1 -> x0, blocking collectives: 6.72 us -> none  [local(): lax.psum((jnp.sum(query_raw * query_raw, axis=1), jnp.sum(key_raw * key_r...]
    another operation x8 -> x0, loops' own time: 5.33 us -> none  [the longest x1 5.16 us: local(): stacked, carried = lax.fori_loop(1, slabs, pass_step, (stacked, carried))]
    ppermute x8 -> x0, starting transfers between devices: 5.28 us -> none  [passed_along(): return lax.ppermute(block, axis, route)]
  transfers between devices with their start and end apart: 9 -> 0, of which waited for: 9 -> 0; matrix products, arithmetic and copies ran while one was open for 1% -> 0% of each run, Pallas kernels for 0% -> 0%
where the time goes in v1:
time: 54.3 us; the launch traced here: 54 us
  Pallas kernels  45.4 us (84%)
  local copies, waits for them, and re-layouts  7.16 us (13%)
  between operations  0.73 us (1%)
  other arithmetic  0.71 us (1%)
    pallas_call x1, Pallas kernels, local_fused(): pl.pallas_call(block_kernel, out_shape=jax.ShapeDtypeStruct((ROWS, WIDTH)...  45.4 us
    unnamed x12, local copies, waits for them, and re-layouts  5.79 us
    another operation x2, local copies, waits for them, and re-layouts, local_fused(): jnp.stack((q_gain, k_gain))  1.37 us

profile of v1, /device:TPU:0, one launch (start us, length us, event | category | flops | bytes accessed | tf_op | source)
XLA Modules:
  0.0 54.0 jit_solution(9072153609056462752)
XLA Ops:
  0.7 0.7 %stack.10 = f32[1,384]{1,0:T(1,128)S(1)} reshape(f32[384]{0:T(512)} %param.17) | data formatting | bytes 3072 | tf_op jit(solution)/shard_map/stack | solution.py:405
  1.3 0.7 %stack.9 = f32[1,384]{1,0:T(1,128)S(1)} reshape(f32[384]{0:T(512)} %param.16) | data formatting | bytes 3072 | tf_op jit(solution)/shard_map/stack | solution.py:405
  2.0 0.0 copy-start
  2.0 2.0 %copy-done = bf16[1536,3,384]{2,0,1:T(8,128)(2,1)S(1)} copy-done((bf16[1536,3,384]{2,0,1:T(8,128)(2,1)S(1)}, bf16[1536,3,384]{2,0,1:T(8,128)(2,1)}, u32[]{:S(2)}) %copy-start) | copy-done | bytes 3538968
  4.0 0.0 copy-start.1
  4.0 1.3 %copy-done.1 = bf16[384,1536]{1,0:T(8,128)(2,1)S(1)} copy-done((bf16[384,1536]{1,0:T(8,128)(2,1)S(1)}, bf16[384,1536]{1,0:T(8,128)(2,1)}, u32[]{:S(2)}) %copy-start.1) | copy-done | bytes 1179672
  5.3 0.0 copy-start.2
  5.3 1.0 %copy-done.2 = f32[16,3,1536]{2,0,1:T(8,128)S(1)} copy-done((f32[16,3,1536]{2,0,1:T(8,128)S(1)}, f32[16,3,1536]{2,0,1:T(8,128)}, u32[]{:S(2)}) %copy-start.2) | copy-done | bytes 294936
  6.3 0.0 copy-start.3
  6.3 0.9 %copy-done.3 = bf16[192,384]{1,0:T(8,128)(2,1)S(1)} copy-done((bf16[192,384]{1,0:T(8,128)(2,1)S(1)}, bf16[192,384]{1,0:T(8,128)(2,1)}, u32[]{:S(2)}) %copy-start.3) | copy-done | bytes 147480
  7.2 0.0 copy-start.4
  7.2 0.7 %copy-done.4 = s32[4]{0:T(128)S(1)} copy-done((s32[4]{0:T(128)S(1)}, s32[4]{0:T(128)}, u32[]{:S(2)}) %copy-start.4) | copy-done | bytes 40
  7.8 0.0 copy-start.5
  7.8 45.4 %shard_map.91 = bf16[192,384]{1,0:T(8,128)(2,1)S(1)} custom-call(s32[4]{0:T(128)S(1)} %copy-done.4, s32[1]{0:T(128)S(6)} %copy.10.offset_ref, bf16[192,384]{1,0:T(8,128)(2,1)S(1)} %copy-done.3, f32[2,384]{1,0:T(2,128)S(1)} %pad_maximum_fusion.gain_ref, bf16[3,1536,384]{2,1,0:T(8,128)(2,1)S(1)} %bitcast.3, bf16[384,1536]{1,0:T(8,128)(2,1)S(1)} %copy-done.1, ...), custom_call_target="tpu_custom_call" | custom-call | tf_op jit(solution)/shard_map/pallas_call | solution.py:358
  53.3 0.0 copy-done.5
  53.3 0.7 %dynamic-slice_select_fusion = bf16[192,384]{1,0:T(8,128)(2,1)} fusion(bf16[192,384]{1,0:T(8,128)(2,1)S(1)} %shard_map.91, bf16[384,384]{1,0:T(8,128)(2,1)S(1)} %copy-done.5, s32[]{:T(128)S(6)} %select_n.30, pred[]{:T(512)S(6)} %eq.6), kind=kLoop, calls=%fused_computation | loop fusion | flops 73728 | bytes 442373 | tf_op jit(solution)/shard_map/jit(_where)/select_n | solution.py:413
  (1 shorter events, 0.0 us)
Async XLA Ops:
  2.0 2.0 %copy-start = (bf16[1536,3,384]{2,0,1:T(8,128)(2,1)S(1)}, bf16[1536,3,384]{2,0,1:T(8,128)(2,1)}, u32[]{:S(2)}) copy-start(bf16[1536,3,384]{2,0,1:T(8,128)(2,1)} %param.14) | copy-start | bytes 10616836
  4.0 1.3 %copy-start.1 = (bf16[384,1536]{1,0:T(8,128)(2,1)S(1)}, bf16[384,1536]{1,0:T(8,128)(2,1)}, u32[]{:S(2)}) copy-start(bf16[384,1536]{1,0:T(8,128)(2,1)} %wout_hbm.1) | copy-start | bytes 3538948
  5.3 1.0 %copy-start.2 = (f32[16,3,1536]{2,0,1:T(8,128)S(1)}, f32[16,3,1536]{2,0,1:T(8,128)}, u32[]{:S(2)}) copy-start(f32[16,3,1536]{2,0,1:T(8,128)} %param.13) | copy-start | bytes 884740
  6.3 0.9 %copy-start.3 = (bf16[192,384]{1,0:T(8,128)(2,1)S(1)}, bf16[192,384]{1,0:T(8,128)(2,1)}, u32[]{:S(2)}) copy-start(bf16[192,384]{1,0:T(8,128)(2,1)} %lat_ref.1) | copy-start | bytes 442372
  7.2 0.7 %copy-start.4 = (s32[4]{0:T(128)S(1)}, s32[4]{0:T(128)}, u32[]{:S(2)}) copy-start(s32[4]{0:T(128)} %noise_ref.1) | copy-start | bytes 52
  7.8 45.5 %copy-start.5 = (bf16[384,384]{1,0:T(8,128)(2,1)S(1)}, bf16[384,384]{1,0:T(8,128)(2,1)}, u32[]{:S(2)}) copy-start(bf16[384,384]{1,0:T(8,128)(2,1)} %param.10) | copy-start | bytes 884740

commit v2 on v1

--- a/solution.py
+++ b/solution.py
@@ -1,3 +1,4 @@
+import math
 import jax
 import jax.numpy as jnp
 from jax import lax
@@ -116,6 +117,9 @@
 ROWS = 192
 WIDTH = 384
 HEADS_DEV = 3
+PIECES = 2
+VMEM_BYTES = 64 * 1024 * 1024 - 128 * 1024
+PIECE = ROWS // PIECES
 
 
 def arrived(buffer, sem):
@@ -123,7 +127,8 @@
 
 
 def block_kernel(
-    noise_ref, offset_ref, lat_ref, gain_ref, w_hbm, wout_hbm, mod_hbm, out_ref,
+    offset_ref, noise_hbm, lat_hbm, q_gain_hbm, k_gain_hbm, w_hbm, wout_hbm, mod_hbm, out_ref,
+    noise_ref, lat_ref, q_gain, k_gain,
     w_v, wo_v, mod_v, lat_buf, mod_act, raw, stat_buf, stage, q_buf, k_buf, v_buf,
     o_buf, a_buf, p_send, rs_buf, upd, fin,
     load_sem, lat_send, lat_recv, st_send, st_recv, qkv_send, q_recv, k_recv, v_recv,
@@ -149,6 +154,10 @@
         pltpu.make_async_copy(mod_hbm, mod_v, load_sem.at[0]),
         pltpu.make_async_copy(w_hbm, w_v, load_sem.at[1]),
         pltpu.make_async_copy(wout_hbm, wo_v, load_sem.at[2]),
+        pltpu.make_async_copy(lat_hbm, lat_ref, load_sem.at[3]),
+        pltpu.make_async_copy(noise_hbm, noise_ref, load_sem.at[4]),
+        pltpu.make_async_copy(q_gain_hbm, q_gain, load_sem.at[5]),
+        pltpu.make_async_copy(k_gain_hbm, k_gain, load_sem.at[6]),
     ]
     for load in loads:
         load.start()
@@ -172,15 +181,26 @@
             device_id=(q_id, h_id), device_id_type=MESH,
         )
 
-    to_x = remote(lat_ref, lat_buf.at[2], lat_send.at[0], lat_recv.at[2], queue, xnb)
-    to_sib = remote(lat_ref, lat_buf.at[1], lat_send.at[1], lat_recv.at[1], queue, sib)
-    to_x.start()
+    loads[3].wait()
+    pieces = [pl.ds(p * PIECE, PIECE) for p in range(PIECES)]
+    to_x, forward = [], []
+    for p, rows in enumerate(pieces):
+        to_x.append(remote(
+            lat_ref.at[rows], lat_buf.at[2, rows], lat_send.at[0, p], lat_recv.at[2, p], queue, xnb
+        ))
+        to_x[p].start()
+        forward.append(remote(
+            lat_buf.at[2, rows], lat_buf.at[3, rows], lat_send.at[2, p], lat_recv.at[3, p], queue, sib
+        ))
+    to_sib = remote(lat_ref, lat_buf.at[1], lat_send.at[1, 0], lat_recv.at[1, 0], queue, sib)
     to_sib.start()
-    forward = remote(lat_buf.at[2], lat_buf.at[3], lat_send.at[2], lat_recv.at[3], queue, sib)
-    arrived(lat_buf.at[2], lat_recv.at[2])
-    forward.start()
-    arrived(lat_buf.at[1], lat_recv.at[1])
+    for p, rows in enumerate(pieces):
+        arrived(lat_buf.at[2, rows], lat_recv.at[2, p])
+        forward[p].start()
+    arrived(lat_buf.at[1], lat_recv.at[1, 0])
     loads[0].wait()
+    for load in loads[4:]:
+        load.wait()
 
     offset = lax.rem(offset_ref[0], ZS)
 
@@ -188,7 +208,8 @@
         return lax.rem(frame + ZS - offset, ZS)
 
     level = noise_ref[position_of(z)]
-    arrived(lat_buf.at[3], lat_recv.at[3])
+    for p, rows in enumerate(pieces):
+        arrived(lat_buf.at[3, rows], lat_recv.at[3, p])
 
     def block(r):
         return (lat_ref[...] if r == 0 else lat_buf[r]).astype(jnp.float32)
@@ -209,6 +230,25 @@
         mod_act[:, columns(r)] = (normed * (1.0 + scale) + shift).astype(jnp.bfloat16)
 
     loads[1].wait()
+    sends = []
+
+    def send_part(part, buf, recv_sem):
+        for j in range(HEADS_DEV):
+            zt = j + c
+            mine = is_self(zt)
+            src = stage.at[part, j]
+            dst = buf.at[z] if part == 0 else buf.at[0, z]
+            far = remote(src, dst, qkv_send.at[part, j], recv_sem.at[z], zt * 2 + c, swap_head)
+            near = pltpu.make_async_copy(src, dst, recv_sem.at[z])
+            pl.when(mine)(near.start)
+            pl.when(jnp.logical_not(mine))(far.start)
+            sends.append((mine, far))
+
+    values = jnp.dot(mod_act[...], w_v[2], preferred_element_type=jnp.float32)
+    for j in range(HEADS_DEV):
+        stage[2, j] = values[:, j * DH:(j + 1) * DH].astype(jnp.bfloat16)
+    send_part(2, v_buf, v_recv)
+
     sums = []
     for i in range(2):
         projected = jnp.dot(mod_act[...], w_v[i], preferred_element_type=jnp.float32)
@@ -229,25 +269,6 @@
     for copy in stats:
         copy.start()
 
-    sends = []
-
-    def send_part(part, buf, recv_sem):
-        for j in range(HEADS_DEV):
-            zt = j + c
-            mine = is_self(zt)
-            src = stage.at[part, j]
-            dst = buf.at[z] if part == 0 else buf.at[0, z]
-            far = remote(src, dst, qkv_send.at[part, j], recv_sem.at[z], zt * 2 + c, swap_head)
-            near = pltpu.make_async_copy(src, dst, recv_sem.at[z])
-            pl.when(mine)(near.start)
-            pl.when(jnp.logical_not(mine))(far.start)
-            sends.append((mine, far))
-
-    values = jnp.dot(mod_act[...], w_v[2], preferred_element_type=jnp.float32)
-    for j in range(HEADS_DEV):
-        stage[2, j] = values[:, j * DH:(j + 1) * DH].astype(jnp.bfloat16)
-    send_part(2, v_buf, v_recv)
-
     for r in (1, 2, 3):
         arrived(stat_buf.at[r], st_recv.at[r])
     total_sq = stat_buf[0] + stat_buf[1] + stat_buf[2] + stat_buf[3]
@@ -255,9 +276,10 @@
     rates = jnp.transpose(jnp.concatenate([rates] * 16, axis=0))[:ROWS]
     for part, buf, recv_sem in ((1, k_buf, k_recv), (0, q_buf, q_recv)):
         rate = rates[:, part:part + 1]
+        gain = (q_gain, k_gain)[part][...].reshape(1, WIDTH)
         for j in range(HEADS_DEV):
             cols = slice(j * DH, (j + 1) * DH)
-            stage[part, j] = (raw[part, :, cols] * rate * gain_ref[part:part + 1, cols]).astype(jnp.bfloat16)
+            stage[part, j] = (raw[part, :, cols] * rate * gain[:, cols]).astype(jnp.bfloat16)
         send_part(part, buf, recv_sem)
 
     active = jnp.logical_and(z - y >= 0, z - y <= 2)
@@ -293,9 +315,9 @@
             scores = lax.dot_general(
                 q_buf[s], keys, (((1,), (1,)), ((), ())), preferred_element_type=jnp.float32
             )
-            scores = scores * DH ** (-0.5) + bias
+            scores = scores * (DH ** (-0.5) * math.log2(math.e)) + bias
             top = jnp.max(scores, axis=1, keepdims=True)
-            e = jnp.exp(scores - top)
+            e = jnp.exp2(scores - top)
             total = jnp.sum(e, axis=1, keepdims=True)
             added = jnp.dot(e.astype(jnp.bfloat16), vals, preferred_element_type=jnp.float32)
             o_buf[s] = (added / total).astype(jnp.bfloat16)
@@ -320,47 +342,63 @@
     def out_block(r):
         return jnp.dot(attn, wo_v[:, columns(r)], preferred_element_type=jnp.float32)
 
+    def rs_copy(kind, p, q_id, h_id):
+        rows = pieces[p]
+        return remote(
+            p_send.at[kind, rows], rs_buf.at[kind, rows], rs_send.at[kind, p], rs_recv.at[kind, p], q_id, h_id
+        )
+
+    send_a, send_b, send_c, moves = [], [], [], []
     p_send[0] = out_block(3).astype(jnp.bfloat16)
-    send_a = remote(p_send.at[0], rs_buf.at[0], rs_send.at[0], rs_recv.at[0], queue, sib)
-    send_a.start()
+    for p in range(PIECES):
+        send_a.append(rs_copy(0, p, queue, sib))
+        send_a[p].start()
     ahead = out_block(2)
     p_send[1] = out_block(1).astype(jnp.bfloat16)
-    send_b = remote(p_send.at[1], rs_buf.at[1], rs_send.at[1], rs_recv.at[1], queue, sib)
-    send_b.start()
-    arrived(rs_buf.at[0], rs_recv.at[0])
-    p_send[2] = (ahead + rs_buf[0].astype(jnp.float32)).astype(jnp.bfloat16)
-    send_c = remote(p_send.at[2], rs_buf.at[2], rs_send.at[2], rs_recv.at[2], queue, xnb)
-    send_c.start()
+    for p in range(PIECES):
+        send_b.append(rs_copy(1, p, queue, sib))
+        send_b[p].start()
+    for p, rows in enumerate(pieces):
+        arrived(rs_buf.at[0, rows], rs_recv.at[0, p])
+        mine = ahead[p * PIECE:(p + 1) * PIECE]
+        p_send[2, rows] = (mine + rs_buf[0, rows].astype(jnp.float32)).astype(jnp.bfloat16)
+        send_c.append(rs_copy(2, p, queue, xnb))
+        send_c[p].start()
     proj = out_block(0)
-    arrived(rs_buf.at[1], rs_recv.at[1])
+    gate = mod_v[2, pl.ds(level, 1), columns(0)]
+    for p, rows in enumerate(pieces):
+        arrived(rs_buf.at[1, rows], rs_recv.at[1, p])
     proj += rs_buf[1].astype(jnp.float32)
-    gate = mod_v[2, pl.ds(level, 1), columns(0)]
-    arrived(rs_buf.at[2], rs_recv.at[2])
-    proj += rs_buf[2].astype(jnp.float32)
-    upd[...] = (lat_ref[...].astype(jnp.float32) + gate * proj).astype(jnp.bfloat16)
-    move = remote(upd, fin, mv_send, mv_recv, below, head)
-    move.start()
-    for copy in (to_x, to_sib, forward, *stats, send_a, send_b, send_c):
+    for p, rows in enumerate(pieces):
+        arrived(rs_buf.at[2, rows], rs_recv.at[2, p])
+        full = proj[p * PIECE:(p + 1) * PIECE] + rs_buf[2, rows].astype(jnp.float32)
+        upd[rows] = (lat_ref[rows].astype(jnp.float32) + gate * full).astype(jnp.bfloat16)
+        moves.append(remote(upd.at[rows], fin.at[rows], mv_send.at[p], mv_recv.at[p], below, head))
+        moves[p].start()
+    for copy in (*to_x, to_sib, *forward, *stats, *send_a, *send_b, *send_c, *moves):
         copy.wait_send()
     for mine, far in sends:
         pl.when(jnp.logical_not(mine))(far.wait_send)
-    move.wait_send()
-    arrived(fin, mv_recv)
-    out_ref[...] = fin[...]
+    for p, rows in enumerate(pieces):
+        arrived(fin.at[rows], mv_recv.at[p])
+        out_ref[rows] = fin[rows]
 
 
 def local_fused(latents, fresh_frame, noise_level, offset, mod_table, w_qkv, w_out, q_gain, k_gain):
     bf16, f32 = jnp.bfloat16, jnp.float32
     dma = pltpu.SemaphoreType.DMA
-    smem = pl.BlockSpec(memory_space=pltpu.SMEM)
     vmem = pl.BlockSpec(memory_space=pltpu.VMEM)
     hbm = pl.BlockSpec(memory_space=pl.ANY)
     moved = pl.pallas_call(
         block_kernel,
         out_shape=jax.ShapeDtypeStruct((ROWS, WIDTH), bf16),
-        in_specs=[smem, smem, vmem, vmem, hbm, hbm, hbm],
+        in_specs=[pl.BlockSpec(memory_space=pltpu.SMEM)] + [hbm] * 7,
         out_specs=vmem,
         scratch_shapes=[
+            pltpu.SMEM(noise_level.shape, jnp.int32),
+            pltpu.VMEM((ROWS, WIDTH), bf16),
+            pltpu.VMEM((WIDTH,), f32),
+            pltpu.VMEM((WIDTH,), f32),
             pltpu.VMEM((3, D, WIDTH), bf16),
             pltpu.VMEM((WIDTH, D), bf16),
             pltpu.VMEM((3, mod_table.shape[0], D), f32),
@@ -378,9 +416,9 @@
             pltpu.VMEM((3, ROWS, WIDTH), bf16),
             pltpu.VMEM((ROWS, WIDTH), bf16),
             pltpu.VMEM((ROWS, WIDTH), bf16),
-            dma((3,)),
-            dma((3,)),
-            dma((4,)),
+            dma((7,)),
+            dma((3, PIECES)),
+            dma((4, PIECES)),
             dma((4,)),
             dma((4,)),
             dma((3, HEADS_DEV)),
@@ -390,19 +428,20 @@
             dma((2, ZS)),
             dma((ZS,)),
             dma((HEADS_DEV,)),
-            dma((3,)),
-            dma((3,)),
-            dma,
-            dma,
+            dma((3, PIECES)),
+            dma((3, PIECES)),
+            dma((PIECES,)),
+            dma((PIECES,)),
         ],
         compiler_params=pltpu.CompilerParams(
-            collective_id=0, has_side_effects=True, vmem_limit_bytes=48 * 1024 * 1024
+            collective_id=0, has_side_effects=True, vmem_limit_bytes=VMEM_BYTES
         ),
     )(
+        offset,
         noise_level,
-        offset,
         latents,
-        jnp.stack((q_gain, k_gain)),
+        q_gain,
+        k_gain,
         jnp.transpose(w_qkv, (1, 0, 2)),
         w_out,
         jnp.transpose(mod_table, (1, 0, 2)),

time: 54.3 us -> 46.1 us (0.85)
  local copies, waits for them, and re-layouts: 7.16 us -> 0 us
  Pallas kernels: 45.4 us -> 43.6 us
  other arithmetic: 0.71 us -> 1.69 us
    unnamed x12 -> x0, local copies, waits for them, and re-layouts: 5.79 us -> none
    pallas_call x1, Pallas kernels: 45.4 us -> 43.6 us  [local_fused(): pl.pallas_call(block_kernel, out_shape=jax.ShapeDtypeStruct((ROWS, WIDTH)...]
    another operation x2 -> x0, local copies, waits for them, and re-layouts: 1.37 us -> none  [local_fused(): jnp.stack((q_gain, k_gain))]
    select_n x1, other arithmetic: 0.7 us -> 1.69 us  [local_fused(): return jnp.where(my_slab // 2 == entry_slot, fresh_half, moved)]
where the time goes in v2:
time: 46.1 us; the launch traced here: 45.9 us
  Pallas kernels  43.6 us (95%)
  other arithmetic  1.69 us (4%)
  between operations  0.68 us (1%)
    pallas_call x1, Pallas kernels, local_fused(): pl.pallas_call(block_kernel, out_shape=jax.ShapeDtypeStruct((ROWS, WIDTH)...  43.6 us
    select_n x1, other arithmetic, local_fused(): return jnp.where(my_slab // 2 == entry_slot, fresh_half, moved)  1.69 us

profile of v2, /device:TPU:0, one launch (start us, length us, event | category | flops | bytes accessed | tf_op | source)
XLA Modules:
  0.0 45.9 jit_solution(8368227871273140037)
XLA Ops:
  0.7 43.6 %shard_map.91 = bf16[192,384]{1,0:T(8,128)(2,1)} custom-call(s32[1]{0:T(128)S(6)} %copy.10.offset_ref, s32[4]{0:T(128)} %noise_hbm.1, bf16[192,384]{1,0:T(8,128)(2,1)} %lat_hbm.1, f32[384]{0:T(512)} %q_gain_hbm.1, f32[384]{0:T(512)} %k_gain_hbm.1, bf16[3,1536,384]{2,1,0:T(8,128)(2,1)} %bitcast.3, bf16[384,1536]{1,0:T(8,128)(2,1)} %wout_hbm.1, ...), custom_call_target="tpu_custom_call" | custom-call | tf_op jit(solution)/shard_map/pallas_call | solution.py:392
  44.2 1.7 %dynamic-slice_select_fusion = bf16[192,384]{1,0:T(8,128)(2,1)} fusion(bf16[192,384]{1,0:T(8,128)(2,1)} %shard_map.91, bf16[384,384]{1,0:T(8,128)(2,1)} %param.10, s32[]{:T(128)S(6)} %select_n.30, pred[]{:T(512)S(6)} %eq.6), kind=kLoop, calls=%fused_computation | loop fusion | flops 73728 | bytes 442373 | tf_op jit(solution)/shard_map/jit(_where)/select_n | solution.py:452

commit v3 on v2

--- a/solution.py
+++ b/solution.py
@@ -130,7 +130,7 @@
     offset_ref, noise_hbm, lat_hbm, q_gain_hbm, k_gain_hbm, w_hbm, wout_hbm, mod_hbm, out_ref,
     noise_ref, lat_ref, q_gain, k_gain,
     w_v, wo_v, mod_v, lat_buf, mod_act, raw, stat_buf, stage, q_buf, k_buf, v_buf,
-    o_buf, a_buf, p_send, rs_buf, upd, fin,
+    o_buf, a_buf, p_send, rs_buf, s_buf, lat_next,
     load_sem, lat_send, lat_recv, st_send, st_recv, qkv_send, q_recv, k_recv, v_recv,
     f_send, o_send, o_recv, rs_send, rs_recv, mv_send, mv_recv,
 ):
@@ -194,6 +194,8 @@
         ))
     to_sib = remote(lat_ref, lat_buf.at[1], lat_send.at[1, 0], lat_recv.at[1, 0], queue, sib)
     to_sib.start()
+    lat_move = remote(lat_ref, lat_next, mv_send, mv_recv, below, head)
+    lat_move.start()
     for p, rows in enumerate(pieces):
         arrived(lat_buf.at[2, rows], lat_recv.at[2, p])
         forward[p].start()
@@ -296,8 +298,6 @@
                 )
                 copy.start()
                 forwards.append(copy)
-        for s in range(ZS):
-            arrived(q_buf.at[s], q_recv.at[s])
         for buf, recv_sem in ((v_buf, v_recv), (k_buf, k_recv)):
             for s in range(ZS):
                 arrived(buf.at[1, s], recv_sem.at[ZS + s])
@@ -309,23 +309,32 @@
             frame += jnp.where(column >= t * ROWS, 1 if t != ZS else 1 - ZS, 0)
         key_pos = frame - offset
         key_pos = jnp.where(key_pos < 0, key_pos + ZS, key_pos)
+        order = (z, z + 1 - 2 * (z % 2), (z + 2) % ZS, ZS - 1 - z)
+
+        def score_into(i):
+            arrived(q_buf.at[order[i]], q_recv.at[order[i]])
+            s_buf[i % 2] = lax.dot_general(
+                q_buf[order[i]], keys, (((1,), (1,)), ((), ())), preferred_element_type=jnp.float32
+            )
+
         outs = []
-        for s in range(ZS):
+        score_into(0)
+        for i, s in enumerate(order):
+            if i + 1 < ZS:
+                score_into(i + 1)
             bias = jnp.where(key_pos <= position_of(s), 0.0, -1e30)
-            scores = lax.dot_general(
-                q_buf[s], keys, (((1,), (1,)), ((), ())), preferred_element_type=jnp.float32
-            )
-            scores = scores * (DH ** (-0.5) * math.log2(math.e)) + bias
+            scores = s_buf[i % 2] * (DH ** (-0.5) * math.log2(math.e)) + bias
             top = jnp.max(scores, axis=1, keepdims=True)
             e = jnp.exp2(scores - top)
             total = jnp.sum(e, axis=1, keepdims=True)
             added = jnp.dot(e.astype(jnp.bfloat16), vals, preferred_element_type=jnp.float32)
-            o_buf[s] = (added / total).astype(jnp.bfloat16)
-            mine = is_self(s)
+            o_buf[i] = (added / total).astype(jnp.bfloat16)
+            zt = (s + ZS - 1) % ZS
+            mine = is_self(zt)
             far = remote(
-                o_buf.at[s], a_buf.at[slot], o_send.at[s], o_recv.at[slot], s * 2 + c, swap_head
+                o_buf.at[i], a_buf.at[slot], o_send.at[i], o_recv.at[slot], zt * 2 + c, swap_head
             )
-            near = pltpu.make_async_copy(o_buf.at[s], a_buf.at[slot], o_recv.at[slot])
+            near = pltpu.make_async_copy(o_buf.at[i], a_buf.at[slot], o_recv.at[slot])
             pl.when(mine)(near.start)
             pl.when(jnp.logical_not(mine))(far.start)
             outs.append((mine, far))
@@ -348,7 +357,7 @@
             p_send.at[kind, rows], rs_buf.at[kind, rows], rs_send.at[kind, p], rs_recv.at[kind, p], q_id, h_id
         )
 
-    send_a, send_b, send_c, moves = [], [], [], []
+    send_a, send_b, send_c = [], [], []
     p_send[0] = out_block(3).astype(jnp.bfloat16)
     for p in range(PIECES):
         send_a.append(rs_copy(0, p, queue, sib))
@@ -365,23 +374,19 @@
         send_c.append(rs_copy(2, p, queue, xnb))
         send_c[p].start()
     proj = out_block(0)
-    gate = mod_v[2, pl.ds(level, 1), columns(0)]
+    gate = mod_v[2, pl.ds(noise_ref[position_of((z + 1) % ZS)], 1), columns(0)]
+    arrived(lat_next, mv_recv)
     for p, rows in enumerate(pieces):
         arrived(rs_buf.at[1, rows], rs_recv.at[1, p])
     proj += rs_buf[1].astype(jnp.float32)
     for p, rows in enumerate(pieces):
         arrived(rs_buf.at[2, rows], rs_recv.at[2, p])
         full = proj[p * PIECE:(p + 1) * PIECE] + rs_buf[2, rows].astype(jnp.float32)
-        upd[rows] = (lat_ref[rows].astype(jnp.float32) + gate * full).astype(jnp.bfloat16)
-        moves.append(remote(upd.at[rows], fin.at[rows], mv_send.at[p], mv_recv.at[p], below, head))
-        moves[p].start()
-    for copy in (*to_x, to_sib, *forward, *stats, *send_a, *send_b, *send_c, *moves):
+        out_ref[rows] = (lat_next[rows].astype(jnp.float32) + gate * full).astype(jnp.bfloat16)
+    for copy in (*to_x, to_sib, *forward, *stats, *send_a, *send_b, *send_c, lat_move):
         copy.wait_send()
     for mine, far in sends:
         pl.when(jnp.logical_not(mine))(far.wait_send)
-    for p, rows in enumerate(pieces):
-        arrived(fin.at[rows], mv_recv.at[p])
-        out_ref[rows] = fin[rows]
 
 
 def local_fused(latents, fresh_frame, noise_level, offset, mod_table, w_qkv, w_out, q_gain, k_gain):
@@ -414,7 +419,7 @@
             pltpu.VMEM((HEADS_DEV, ROWS, DH), bf16),
             pltpu.VMEM((3, ROWS, WIDTH), bf16),
             pltpu.VMEM((3, ROWS, WIDTH), bf16),
-            pltpu.VMEM((ROWS, WIDTH), bf16),
+            pltpu.VMEM((2, ROWS, 2 * ZS * ROWS), f32),
             pltpu.VMEM((ROWS, WIDTH), bf16),
             dma((7,)),
             dma((3, PIECES)),
@@ -430,8 +435,8 @@
             dma((HEADS_DEV,)),
             dma((3, PIECES)),
             dma((3, PIECES)),
-            dma((PIECES,)),
-            dma((PIECES,)),
+            dma,
+            dma,
         ],
         compiler_params=pltpu.CompilerParams(
             collective_id=0, has_side_effects=True, vmem_limit_bytes=VMEM_BYTES

time: 46.1 us -> 41.3 us (0.90)
  Pallas kernels: 43.6 us -> 38.7 us
    pallas_call x1, Pallas kernels: 43.6 us -> 38.7 us  [local_fused(): pl.pallas_call(block_kernel, out_shape=jax.ShapeDtypeStruct((ROWS, WIDTH)...]
where the time goes in v3:
time: 41.3 us; the launch traced here: 41.1 us
  Pallas kernels  38.7 us (94%)
  other arithmetic  1.69 us (4%)
  between operations  0.68 us (2%)
    pallas_call x1, Pallas kernels, local_fused(): pl.pallas_call(block_kernel, out_shape=jax.ShapeDtypeStruct((ROWS, WIDTH)...  38.7 us
    select_n x1, other arithmetic, local_fused(): return jnp.where(my_slab // 2 == entry_slot, fresh_half, moved)  1.69 us

profile of v3, /device:TPU:0, one launch (start us, length us, event | category | flops | bytes accessed | tf_op | source)
XLA Modules:
  0.0 41.1 jit_solution(8423958110391531206)
XLA Ops:
  0.7 38.7 %shard_map.91 = bf16[192,384]{1,0:T(8,128)(2,1)} custom-call(s32[1]{0:T(128)S(6)} %copy.10.offset_ref, s32[4]{0:T(128)} %noise_hbm.1, bf16[192,384]{1,0:T(8,128)(2,1)} %lat_hbm.1, f32[384]{0:T(512)} %q_gain_hbm.1, f32[384]{0:T(512)} %k_gain_hbm.1, bf16[3,1536,384]{2,1,0:T(8,128)(2,1)} %bitcast.3, bf16[384,1536]{1,0:T(8,128)(2,1)} %wout_hbm.1, ...), custom_call_target="tpu_custom_call" | custom-call | tf_op jit(solution)/shard_map/pallas_call | solution.py:397
  39.4 1.7 %dynamic-slice_select_fusion = bf16[192,384]{1,0:T(8,128)(2,1)} fusion(bf16[192,384]{1,0:T(8,128)(2,1)} %shard_map.91, bf16[384,384]{1,0:T(8,128)(2,1)} %param.10, s32[]{:T(128)S(6)} %select_n.30, pred[]{:T(512)S(6)} %eq.6), kind=kLoop, calls=%fused_computation | loop fusion | flops 73728 | bytes 442373 | tf_op jit(solution)/shard_map/jit(_where)/select_n | solution.py:457

commit v4 on v3

--- a/solution.py
+++ b/solution.py
@@ -130,9 +130,9 @@
     offset_ref, noise_hbm, lat_hbm, q_gain_hbm, k_gain_hbm, w_hbm, wout_hbm, mod_hbm, out_ref,
     noise_ref, lat_ref, q_gain, k_gain,
     w_v, wo_v, mod_v, lat_buf, mod_act, raw, stat_buf, stage, q_buf, k_buf, v_buf,
-    o_buf, a_buf, p_send, rs_buf, s_buf, lat_next,
+    o_buf, a_buf, w_col, s_buf, lat_next,
     load_sem, lat_send, lat_recv, st_send, st_recv, qkv_send, q_recv, k_recv, v_recv,
-    f_send, o_send, o_recv, rs_send, rs_recv, mv_send, mv_recv,
+    f_send, o_send, o_recv, a_send, w_send, w_recv, mv_send, mv_recv,
 ):
     queue = lax.axis_index("queue")
     head = lax.axis_index("head")
@@ -145,6 +145,7 @@
     below = queue - 2 + jnp.where(z == 0, 2 * ZS, 0)
     above = queue + 2 - jnp.where(z == ZS - 1, 2 * ZS, 0)
     swap_head = x * 2 + y
+    swap_other = (1 - x) * 2 + y
     on_diagonal = y == c
 
     def is_self(zt):
@@ -173,7 +174,8 @@
     greet(above, head)
     for zt in range(ZS):
         pl.when(jnp.logical_not(is_self(zt)))(lambda zt=zt: greet(zt * 2 + c, swap_head))
-    pl.semaphore_wait(barrier, 5 + ZS - jnp.where(on_diagonal, 1, 0))
+        greet(zt * 2 + c, swap_other)
+    pl.semaphore_wait(barrier, 5 + 2 * ZS - jnp.where(on_diagonal, 1, 0))
 
     def remote(src, dst, s_sem, r_sem, q_id, h_id):
         return pltpu.make_async_remote_copy(
@@ -219,6 +221,18 @@
     def columns(r):
         return pl.ds(pl.multiple_of(peers[r] * WIDTH, WIDTH), WIDTH)
 
+    loads[2].wait()
+    weights = []
+
+    def send_weights(r, part):
+        rows = pl.ds(part * (WIDTH // 2), WIDTH // 2)
+        copy = remote(
+            wo_v.at[rows, columns(r)], w_col.at[r, rows], w_send.at[r, part], w_recv.at[r, part], queue, peers[r]
+        )
+        copy.start()
+        weights.append(copy)
+
+    send_weights(3, 0)
     mean = sum(jnp.sum(block(r), axis=1, keepdims=True) for r in range(4)) / D
     square = jnp.zeros((ROWS, 1), jnp.float32)
     for r in range(4):
@@ -283,6 +297,11 @@
             cols = slice(j * DH, (j + 1) * DH)
             stage[part, j] = (raw[part, :, cols] * rate * gain[:, cols]).astype(jnp.bfloat16)
         send_part(part, buf, recv_sem)
+
+    send_weights(3, 1)
+    for r in (2, 1):
+        for part in range(2):
+            send_weights(r, part)
 
     active = jnp.logical_and(z - y >= 0, z - y <= 2)
     slot = jnp.where(active, z - y, 0)
@@ -332,9 +351,14 @@
             zt = (s + ZS - 1) % ZS
             mine = is_self(zt)
             far = remote(
-                o_buf.at[i], a_buf.at[slot], o_send.at[i], o_recv.at[slot], zt * 2 + c, swap_head
+                o_buf.at[i], a_buf.at[0, slot], o_send.at[0, i], o_recv.at[0, slot], zt * 2 + c, swap_head
             )
-            near = pltpu.make_async_copy(o_buf.at[i], a_buf.at[slot], o_recv.at[slot])
+            near = pltpu.make_async_copy(o_buf.at[i], a_buf.at[0, slot], o_recv.at[0, slot])
+            other = remote(
+                o_buf.at[i], a_buf.at[2, slot], o_send.at[1, i], o_recv.at[2, slot], zt * 2 + c, swap_other
+            )
+            other.start()
+            forwards.append(other)
             pl.when(mine)(near.start)
             pl.when(jnp.logical_not(mine))(far.start)
             outs.append((mine, far))
@@ -343,47 +367,35 @@
         for mine, far in outs:
             pl.when(jnp.logical_not(mine))(far.wait_send)
 
-    loads[2].wait()
+    shared = []
     for j in range(HEADS_DEV):
-        arrived(a_buf.at[j], o_recv.at[j])
-    attn = jnp.concatenate([a_buf[j] for j in range(HEADS_DEV)], axis=1)
+        for r in (0, 2):
+            arrived(a_buf.at[r, j], o_recv.at[r, j])
+            copy = remote(
+                a_buf.at[r, j], a_buf.at[r + 1, j], a_send.at[r // 2, j], o_recv.at[r + 1, j], queue, sib
+            )
+            copy.start()
+            shared.append(copy)
 
     def out_block(r):
-        return jnp.dot(attn, wo_v[:, columns(r)], preferred_element_type=jnp.float32)
-
-    def rs_copy(kind, p, q_id, h_id):
-        rows = pieces[p]
-        return remote(
-            p_send.at[kind, rows], rs_buf.at[kind, rows], rs_send.at[kind, p], rs_recv.at[kind, p], q_id, h_id
-        )
-
-    send_a, send_b, send_c = [], [], []
-    p_send[0] = out_block(3).astype(jnp.bfloat16)
-    for p in range(PIECES):
-        send_a.append(rs_copy(0, p, queue, sib))
-        send_a[p].start()
-    ahead = out_block(2)
-    p_send[1] = out_block(1).astype(jnp.bfloat16)
-    for p in range(PIECES):
-        send_b.append(rs_copy(1, p, queue, sib))
-        send_b[p].start()
-    for p, rows in enumerate(pieces):
-        arrived(rs_buf.at[0, rows], rs_recv.at[0, p])
-        mine = ahead[p * PIECE:(p + 1) * PIECE]
-        p_send[2, rows] = (mine + rs_buf[0, rows].astype(jnp.float32)).astype(jnp.bfloat16)
-        send_c.append(rs_copy(2, p, queue, xnb))
-        send_c[p].start()
+        attn = jnp.concatenate([a_buf[r, j] for j in range(HEADS_DEV)], axis=1)
+        own = wo_v[:, columns(0)] if r == 0 else w_col[r]
+        return jnp.dot(attn, own, preferred_element_type=jnp.float32)
+
     proj = out_block(0)
+    for r in (1, 2, 3):
+        for part in range(2):
+            rows = pl.ds(part * (WIDTH // 2), WIDTH // 2)
+            arrived(w_col.at[r, rows], w_recv.at[r, part])
+    proj += out_block(2)
     gate = mod_v[2, pl.ds(noise_ref[position_of((z + 1) % ZS)], 1), columns(0)]
     arrived(lat_next, mv_recv)
-    for p, rows in enumerate(pieces):
-        arrived(rs_buf.at[1, rows], rs_recv.at[1, p])
-    proj += rs_buf[1].astype(jnp.float32)
-    for p, rows in enumerate(pieces):
-        arrived(rs_buf.at[2, rows], rs_recv.at[2, p])
-        full = proj[p * PIECE:(p + 1) * PIECE] + rs_buf[2, rows].astype(jnp.float32)
-        out_ref[rows] = (lat_next[rows].astype(jnp.float32) + gate * full).astype(jnp.bfloat16)
-    for copy in (*to_x, to_sib, *forward, *stats, *send_a, *send_b, *send_c, lat_move):
+    for r in (1, 3):
+        for j in range(HEADS_DEV):
+            arrived(a_buf.at[r, j], o_recv.at[r, j])
+        proj += out_block(r)
+    out_ref[...] = (lat_next[...].astype(jnp.float32) + gate * proj).astype(jnp.bfloat16)
+    for copy in (*to_x, to_sib, *forward, *stats, *weights, *shared, lat_move):
         copy.wait_send()
     for mine, far in sends:
         pl.when(jnp.logical_not(mine))(far.wait_send)
@@ -416,9 +428,8 @@
             pltpu.VMEM((2, ZS, ROWS, DH), bf16),
             pltpu.VMEM((2, ZS, ROWS, DH), bf16),
             pltpu.VMEM((ZS, ROWS, DH), bf16),
-            pltpu.VMEM((HEADS_DEV, ROWS, DH), bf16),
-            pltpu.VMEM((3, ROWS, WIDTH), bf16),
-            pltpu.VMEM((3, ROWS, WIDTH), bf16),
+            pltpu.VMEM((4, HEADS_DEV, ROWS, DH), bf16),
+            pltpu.VMEM((4, WIDTH, WIDTH), bf16),
             pltpu.VMEM((2, ROWS, 2 * ZS * ROWS), f32),
             pltpu.VMEM((ROWS, WIDTH), bf16),
             dma((7,)),
@@ -431,10 +442,11 @@
             dma((2 * ZS,)),
             dma((2 * ZS,)),
             dma((2, ZS)),
-            dma((ZS,)),
-            dma((HEADS_DEV,)),
-            dma((3, PIECES)),
-            dma((3, PIECES)),
+            dma((2, ZS)),
+            dma((4, HEADS_DEV)),
+            dma((2, HEADS_DEV)),
+            dma((4, 2)),
+            dma((4, 2)),
             dma,
             dma,
         ],

time: 41.3 us -> 41.7 us (level)
  Pallas kernels: 38.7 us -> 39.3 us
    pallas_call x1, Pallas kernels: 38.7 us -> 39.3 us  [local_fused(): pl.pallas_call(block_kernel, out_shape=jax.ShapeDtypeStruct((ROWS, WIDTH)...]
where the time goes in v4:
time: 41.7 us; the launch traced here: 41.6 us
  Pallas kernels  39.3 us (94%)
  other arithmetic  1.62 us (4%)
  between operations  0.68 us (2%)
    pallas_call x1, Pallas kernels, local_fused(): pl.pallas_call(block_kernel, out_shape=jax.ShapeDtypeStruct((ROWS, WIDTH)...  39.3 us
    select_n x1, other arithmetic, local_fused(): return jnp.where(my_slab // 2 == entry_slot, fresh_half, moved)  1.62 us

profile of v4, /device:TPU:0, one launch (start us, length us, event | category | flops | bytes accessed | tf_op | source)
XLA Modules:
  0.0 41.6 jit_solution(11018715128169604111)
XLA Ops:
  0.7 39.3 %shard_map.91 = bf16[192,384]{1,0:T(8,128)(2,1)} custom-call(s32[1]{0:T(128)S(6)} %copy.10.offset_ref, s32[4]{0:T(128)} %noise_hbm.1, bf16[192,384]{1,0:T(8,128)(2,1)} %lat_hbm.1, f32[384]{0:T(512)} %q_gain_hbm.1, f32[384]{0:T(512)} %k_gain_hbm.1, bf16[3,1536,384]{2,1,0:T(8,128)(2,1)} %bitcast.3, bf16[384,1536]{1,0:T(8,128)(2,1)} %wout_hbm.1, ...), custom_call_target="tpu_custom_call" | custom-call | tf_op jit(solution)/shard_map/pallas_call | solution.py:409
  39.9 1.6 %dynamic-slice_select_fusion = bf16[192,384]{1,0:T(8,128)(2,1)} fusion(bf16[192,384]{1,0:T(8,128)(2,1)} %shard_map.91, bf16[384,384]{1,0:T(8,128)(2,1)} %param.10, s32[]{:T(128)S(6)} %select_n.30, pred[]{:T(512)S(6)} %eq.6), kind=kLoop, calls=%fused_computation | loop fusion | flops 73728 | bytes 442373 | tf_op jit(solution)/shard_map/jit(_where)/select_n | solution.py:469

commit v5 on v3

--- a/solution.py
+++ b/solution.py
@@ -183,23 +183,28 @@
 
     loads[3].wait()
     pieces = [pl.ds(p * PIECE, PIECE) for p in range(PIECES)]
-    to_x, forward = [], []
+    to_x, to_sib, forward, stats, sends = [], [], [], [], []
     for p, rows in enumerate(pieces):
         to_x.append(remote(
             lat_ref.at[rows], lat_buf.at[2, rows], lat_send.at[0, p], lat_recv.at[2, p], queue, xnb
         ))
         to_x[p].start()
+    for p, rows in enumerate(pieces):
+        to_sib.append(remote(
+            lat_ref.at[rows], lat_buf.at[1, rows], lat_send.at[1, p], lat_recv.at[1, p], queue, sib
+        ))
+        to_sib[p].start()
         forward.append(remote(
             lat_buf.at[2, rows], lat_buf.at[3, rows], lat_send.at[2, p], lat_recv.at[3, p], queue, sib
         ))
-    to_sib = remote(lat_ref, lat_buf.at[1], lat_send.at[1, 0], lat_recv.at[1, 0], queue, sib)
-    to_sib.start()
+
+    def pass_latents(p):
+        arrived(lat_buf.at[2, pieces[p]], lat_recv.at[2, p])
+        forward[p].start()
+
+    pass_latents(0)
     lat_move = remote(lat_ref, lat_next, mv_send, mv_recv, below, head)
     lat_move.start()
-    for p, rows in enumerate(pieces):
-        arrived(lat_buf.at[2, rows], lat_recv.at[2, p])
-        forward[p].start()
-    arrived(lat_buf.at[1], lat_recv.at[1, 0])
     loads[0].wait()
     for load in loads[4:]:
         load.wait()
@@ -210,79 +215,97 @@
         return lax.rem(frame + ZS - offset, ZS)
 
     level = noise_ref[position_of(z)]
-    for p, rows in enumerate(pieces):
-        arrived(lat_buf.at[3, rows], lat_recv.at[3, p])
-
-    def block(r):
-        return (lat_ref[...] if r == 0 else lat_buf[r]).astype(jnp.float32)
 
     def columns(r):
         return pl.ds(pl.multiple_of(peers[r] * WIDTH, WIDTH), WIDTH)
 
-    mean = sum(jnp.sum(block(r), axis=1, keepdims=True) for r in range(4)) / D
-    square = jnp.zeros((ROWS, 1), jnp.float32)
-    for r in range(4):
-        centered = block(r) - mean
-        square += jnp.sum(centered * centered, axis=1, keepdims=True)
-    inv = lax.rsqrt(square / D + 1e-06)
-    for r in range(4):
-        shift = mod_v[0, pl.ds(level, 1), columns(r)]
-        scale = mod_v[1, pl.ds(level, 1), columns(r)]
-        normed = (block(r) - mean) * inv
-        mod_act[:, columns(r)] = (normed * (1.0 + scale) + shift).astype(jnp.bfloat16)
-
-    loads[1].wait()
-    sends = []
-
-    def send_part(part, buf, recv_sem):
+    def norm_piece(p):
+        rows = pieces[p]
+        for r in (1, 3):
+            arrived(lat_buf.at[r, rows], lat_recv.at[r, p])
+
+        def block(r):
+            return (lat_ref[rows] if r == 0 else lat_buf[r, rows]).astype(jnp.float32)
+
+        mean = sum(jnp.sum(block(r), axis=1, keepdims=True) for r in range(4)) / D
+        square = jnp.zeros((PIECE, 1), jnp.float32)
+        for r in range(4):
+            centered = block(r) - mean
+            square += jnp.sum(centered * centered, axis=1, keepdims=True)
+        inv = lax.rsqrt(square / D + 1e-06)
+        for r in range(4):
+            shift = mod_v[0, pl.ds(level, 1), columns(r)]
+            scale = mod_v[1, pl.ds(level, 1), columns(r)]
+            normed = (block(r) - mean) * inv
+            mod_act[rows, columns(r)] = (normed * (1.0 + scale) + shift).astype(jnp.bfloat16)
+
+    def send_part(part, p, buf, recv_sem):
+        rows = pieces[p]
         for j in range(HEADS_DEV):
             zt = j + c
             mine = is_self(zt)
-            src = stage.at[part, j]
-            dst = buf.at[z] if part == 0 else buf.at[0, z]
-            far = remote(src, dst, qkv_send.at[part, j], recv_sem.at[z], zt * 2 + c, swap_head)
+            src = stage.at[part, j, rows]
+            dst = buf.at[z, rows] if part == 0 else buf.at[0, z, rows]
+            far = remote(src, dst, qkv_send.at[part, j, p], recv_sem.at[z], zt * 2 + c, swap_head)
             near = pltpu.make_async_copy(src, dst, recv_sem.at[z])
             pl.when(mine)(near.start)
             pl.when(jnp.logical_not(mine))(far.start)
             sends.append((mine, far))
 
-    values = jnp.dot(mod_act[...], w_v[2], preferred_element_type=jnp.float32)
-    for j in range(HEADS_DEV):
-        stage[2, j] = values[:, j * DH:(j + 1) * DH].astype(jnp.bfloat16)
-    send_part(2, v_buf, v_recv)
-
-    sums = []
-    for i in range(2):
-        projected = jnp.dot(mod_act[...], w_v[i], preferred_element_type=jnp.float32)
-        raw[i] = projected
-        sums.append(jnp.sum(projected * projected, axis=1, keepdims=True))
-    lane = lax.broadcasted_iota(jnp.int32, (256, 128), 1)
-    padding = jnp.zeros((256 - ROWS, 1), jnp.float32)
-    spread = jnp.where(
-        lane == 0,
-        jnp.concatenate([sums[0], padding], axis=0),
-        jnp.concatenate([sums[1], padding], axis=0),
-    )
-    stat_buf[0] = jnp.transpose(spread)[:8]
-    stats = [
-        remote(stat_buf.at[0], stat_buf.at[r], st_send.at[r], st_recv.at[r], queue, peers[r])
-        for r in (2, 3, 1)
-    ]
-    for copy in stats:
-        copy.start()
-
-    for r in (1, 2, 3):
-        arrived(stat_buf.at[r], st_recv.at[r])
-    total_sq = stat_buf[0] + stat_buf[1] + stat_buf[2] + stat_buf[3]
-    rates = lax.rsqrt(total_sq / D + 1e-06)
-    rates = jnp.transpose(jnp.concatenate([rates] * 16, axis=0))[:ROWS]
-    for part, buf, recv_sem in ((1, k_buf, k_recv), (0, q_buf, q_recv)):
-        rate = rates[:, part:part + 1]
-        gain = (q_gain, k_gain)[part][...].reshape(1, WIDTH)
+    def project_values(p):
+        rows = pieces[p]
+        values = jnp.dot(mod_act[rows], w_v[2], preferred_element_type=jnp.float32)
         for j in range(HEADS_DEV):
-            cols = slice(j * DH, (j + 1) * DH)
-            stage[part, j] = (raw[part, :, cols] * rate * gain[:, cols]).astype(jnp.bfloat16)
-        send_part(part, buf, recv_sem)
+            stage[2, j, rows] = values[:, j * DH:(j + 1) * DH].astype(jnp.bfloat16)
+        send_part(2, p, v_buf, v_recv)
+
+    def project_keys(p):
+        rows = pieces[p]
+        sums = []
+        for i in range(2):
+            projected = jnp.dot(mod_act[rows], w_v[i], preferred_element_type=jnp.float32)
+            raw[i, rows] = projected
+            sums.append(jnp.sum(projected * projected, axis=1, keepdims=True))
+        lane = lax.broadcasted_iota(jnp.int32, (128, 128), 1)
+        padding = jnp.zeros((128 - PIECE, 1), jnp.float32)
+        spread = jnp.where(
+            lane == 0,
+            jnp.concatenate([sums[0], padding], axis=0),
+            jnp.concatenate([sums[1], padding], axis=0),
+        )
+        stat_buf[p, 0] = jnp.transpose(spread)[:8]
+        for r in (2, 3, 1):
+            copy = remote(
+                stat_buf.at[p, 0], stat_buf.at[p, r], st_send.at[p, r], st_recv.at[p, r], queue, peers[r]
+            )
+            copy.start()
+            stats.append(copy)
+
+    def send_keys(p):
+        rows = pieces[p]
+        for r in (1, 2, 3):
+            arrived(stat_buf.at[p, r], st_recv.at[p, r])
+        total_sq = stat_buf[p, 0] + stat_buf[p, 1] + stat_buf[p, 2] + stat_buf[p, 3]
+        rates = lax.rsqrt(total_sq / D + 1e-06)
+        rates = jnp.transpose(jnp.concatenate([rates] * 16, axis=0))[:PIECE]
+        for part, buf, recv_sem in ((1, k_buf, k_recv), (0, q_buf, q_recv)):
+            rate = rates[:, part:part + 1]
+            gain = (q_gain, k_gain)[part][...].reshape(1, WIDTH)
+            for j in range(HEADS_DEV):
+                cols = slice(j * DH, (j + 1) * DH)
+                stage[part, j, rows] = (raw[part, rows, cols] * rate * gain[:, cols]).astype(jnp.bfloat16)
+            send_part(part, p, buf, recv_sem)
+
+    norm_piece(0)
+    loads[1].wait()
+    project_values(0)
+    pass_latents(1)
+    project_keys(0)
+    norm_piece(1)
+    project_values(1)
+    project_keys(1)
+    send_keys(0)
+    send_keys(1)
 
     active = jnp.logical_and(z - y >= 0, z - y <= 2)
     slot = jnp.where(active, z - y, 0)
@@ -383,7 +406,7 @@
         arrived(rs_buf.at[2, rows], rs_recv.at[2, p])
         full = proj[p * PIECE:(p + 1) * PIECE] + rs_buf[2, rows].astype(jnp.float32)
         out_ref[rows] = (lat_next[rows].astype(jnp.float32) + gate * full).astype(jnp.bfloat16)
-    for copy in (*to_x, to_sib, *forward, *stats, *send_a, *send_b, *send_c, lat_move):
+    for copy in (*to_x, *to_sib, *forward, *stats, *send_a, *send_b, *send_c, lat_move):
         copy.wait_send()
     for mine, far in sends:
         pl.when(jnp.logical_not(mine))(far.wait_send)
@@ -410,7 +433,7 @@
             pltpu.VMEM((4, ROWS, WIDTH), bf16),
             pltpu.VMEM((ROWS, D), bf16),
             pltpu.VMEM((2, ROWS, WIDTH), f32),
-            pltpu.VMEM((4, 8, 256), f32),
+            pltpu.VMEM((PIECES, 4, 8, 128), f32),
             pltpu.VMEM((3, HEADS_DEV, ROWS, DH), bf16),
             pltpu.VMEM((ZS, ROWS, DH), bf16),
             pltpu.VMEM((2, ZS, ROWS, DH), bf16),
@@ -424,9 +447,9 @@
             dma((7,)),
             dma((3, PIECES)),
             dma((4, PIECES)),
-            dma((4,)),
-            dma((4,)),
-            dma((3, HEADS_DEV)),
+            dma((PIECES, 4)),
+            dma((PIECES, 4)),
+            dma((3, HEADS_DEV, PIECES)),
             dma((ZS,)),
             dma((2 * ZS,)),
             dma((2 * ZS,)),

time: 41.3 us -> 42.9 us (1.039)
  Pallas kernels: 38.7 us -> 40.4 us
    pallas_call x1, Pallas kernels: 38.7 us -> 40.4 us  [local_fused(): pl.pallas_call(block_kernel, out_shape=jax.ShapeDtypeStruct((ROWS, WIDTH)...]
where the time goes in v5:
time: 42.9 us; the launch traced here: 42.7 us
  Pallas kernels  40.4 us (94%)
  other arithmetic  1.69 us (4%)
  between operations  0.68 us (2%)
    pallas_call x1, Pallas kernels, local_fused(): pl.pallas_call(block_kernel, out_shape=jax.ShapeDtypeStruct((ROWS, WIDTH)...  40.4 us
    select_n x1, other arithmetic, local_fused(): return jnp.where(my_slab // 2 == entry_slot, fresh_half, moved)  1.69 us

profile of v5, /device:TPU:0, one launch (start us, length us, event | category | flops | bytes accessed | tf_op | source)
XLA Modules:
  0.0 42.7 jit_solution(8428890566600907899)
XLA Ops:
  0.7 40.4 %shard_map.91 = bf16[192,384]{1,0:T(8,128)(2,1)} custom-call(s32[1]{0:T(128)S(6)} %copy.10.offset_ref, s32[4]{0:T(128)} %noise_hbm.1, bf16[192,384]{1,0:T(8,128)(2,1)} %lat_hbm.1, f32[384]{0:T(512)} %q_gain_hbm.1, f32[384]{0:T(512)} %k_gain_hbm.1, bf16[3,1536,384]{2,1,0:T(8,128)(2,1)} %bitcast.3, bf16[384,1536]{1,0:T(8,128)(2,1)} %wout_hbm.1, ...), custom_call_target="tpu_custom_call" | custom-call | tf_op jit(solution)/shard_map/pallas_call | solution.py:420
  41.1 1.7 %dynamic-slice_select_fusion = bf16[192,384]{1,0:T(8,128)(2,1)} fusion(bf16[192,384]{1,0:T(8,128)(2,1)} %shard_map.91, bf16[384,384]{1,0:T(8,128)(2,1)} %param.10, s32[]{:T(128)S(6)} %select_n.30, pred[]{:T(512)S(6)} %eq.6), kind=kLoop, calls=%fused_computation | loop fusion | flops 73728 | bytes 442373 | tf_op jit(solution)/shard_map/jit(_where)/select_n | solution.py:480

commit v6 on v3

--- a/solution.py
+++ b/solution.py
@@ -129,9 +129,9 @@
 def block_kernel(
     offset_ref, noise_hbm, lat_hbm, q_gain_hbm, k_gain_hbm, w_hbm, wout_hbm, mod_hbm, out_ref,
     noise_ref, lat_ref, q_gain, k_gain,
-    w_v, wo_v, mod_v, lat_buf, mod_act, raw, stat_buf, stage, q_buf, k_buf, v_buf,
+    w_v, wo_v, mod_v, lat_buf, mod_act, raw, stat_buf, stage_kq, stage_v, kq_buf, v_buf, k_sib, v_sib,
     o_buf, a_buf, p_send, rs_buf, s_buf, lat_next,
-    load_sem, lat_send, lat_recv, st_send, st_recv, qkv_send, q_recv, k_recv, v_recv,
+    load_sem, lat_send, lat_recv, st_send, st_recv, qkv_send, kq_recv, v_recv, ks_recv, vs_recv,
     f_send, o_send, o_recv, rs_send, rs_recv, mv_send, mv_recv,
 ):
     queue = lax.axis_index("queue")
@@ -183,23 +183,16 @@
 
     loads[3].wait()
     pieces = [pl.ds(p * PIECE, PIECE) for p in range(PIECES)]
-    to_x, forward = [], []
-    for p, rows in enumerate(pieces):
-        to_x.append(remote(
-            lat_ref.at[rows], lat_buf.at[2, rows], lat_send.at[0, p], lat_recv.at[2, p], queue, xnb
-        ))
-        to_x[p].start()
-        forward.append(remote(
-            lat_buf.at[2, rows], lat_buf.at[3, rows], lat_send.at[2, p], lat_recv.at[3, p], queue, sib
-        ))
-    to_sib = remote(lat_ref, lat_buf.at[1], lat_send.at[1, 0], lat_recv.at[1, 0], queue, sib)
+    to_x = remote(lat_ref, lat_buf.at[2], lat_send.at[0], lat_recv.at[2], queue, xnb)
+    to_x.start()
+    to_sib = remote(lat_ref, lat_buf.at[1], lat_send.at[1], lat_recv.at[1], queue, sib)
     to_sib.start()
     lat_move = remote(lat_ref, lat_next, mv_send, mv_recv, below, head)
     lat_move.start()
-    for p, rows in enumerate(pieces):
-        arrived(lat_buf.at[2, rows], lat_recv.at[2, p])
-        forward[p].start()
-    arrived(lat_buf.at[1], lat_recv.at[1, 0])
+    forward = remote(lat_buf.at[2], lat_buf.at[3], lat_send.at[2], lat_recv.at[3], queue, sib)
+    arrived(lat_buf.at[2], lat_recv.at[2])
+    forward.start()
+    arrived(lat_buf.at[1], lat_recv.at[1])
     loads[0].wait()
     for load in loads[4:]:
         load.wait()
@@ -210,8 +203,7 @@
         return lax.rem(frame + ZS - offset, ZS)
 
     level = noise_ref[position_of(z)]
-    for p, rows in enumerate(pieces):
-        arrived(lat_buf.at[3, rows], lat_recv.at[3, p])
+    arrived(lat_buf.at[3], lat_recv.at[3])
 
     def block(r):
         return (lat_ref[...] if r == 0 else lat_buf[r]).astype(jnp.float32)
@@ -238,17 +230,16 @@
         for j in range(HEADS_DEV):
             zt = j + c
             mine = is_self(zt)
-            src = stage.at[part, j]
-            dst = buf.at[z] if part == 0 else buf.at[0, z]
-            far = remote(src, dst, qkv_send.at[part, j], recv_sem.at[z], zt * 2 + c, swap_head)
-            near = pltpu.make_async_copy(src, dst, recv_sem.at[z])
+            src = stage_v.at[j] if part == 2 else stage_kq.at[j]
+            far = remote(src, buf.at[z], qkv_send.at[part, j], recv_sem.at[z], zt * 2 + c, swap_head)
+            near = pltpu.make_async_copy(src, buf.at[z], recv_sem.at[z])
             pl.when(mine)(near.start)
             pl.when(jnp.logical_not(mine))(far.start)
             sends.append((mine, far))
 
     values = jnp.dot(mod_act[...], w_v[2], preferred_element_type=jnp.float32)
     for j in range(HEADS_DEV):
-        stage[2, j] = values[:, j * DH:(j + 1) * DH].astype(jnp.bfloat16)
+        stage_v[j] = values[:, j * DH:(j + 1) * DH].astype(jnp.bfloat16)
     send_part(2, v_buf, v_recv)
 
     sums = []
@@ -276,45 +267,49 @@
     total_sq = stat_buf[0] + stat_buf[1] + stat_buf[2] + stat_buf[3]
     rates = lax.rsqrt(total_sq / D + 1e-06)
     rates = jnp.transpose(jnp.concatenate([rates] * 16, axis=0))[:ROWS]
-    for part, buf, recv_sem in ((1, k_buf, k_recv), (0, q_buf, q_recv)):
+    for part in range(2):
         rate = rates[:, part:part + 1]
         gain = (q_gain, k_gain)[part][...].reshape(1, WIDTH)
         for j in range(HEADS_DEV):
             cols = slice(j * DH, (j + 1) * DH)
-            stage[part, j] = (raw[part, :, cols] * rate * gain[:, cols]).astype(jnp.bfloat16)
-        send_part(part, buf, recv_sem)
+            stage_kq[j, part] = (raw[part, :, cols] * rate * gain[:, cols]).astype(jnp.bfloat16)
+    send_part(1, kq_buf, kq_recv)
 
     active = jnp.logical_and(z - y >= 0, z - y <= 2)
     slot = jnp.where(active, z - y, 0)
 
     @pl.when(active)
     def _():
-        forwards = []
-        for kind, (buf, recv_sem) in enumerate(((v_buf, v_recv), (k_buf, k_recv))):
-            for s in range(ZS):
-                arrived(buf.at[0, s], recv_sem.at[s])
-                copy = remote(
-                    buf.at[0, s], buf.at[1, s], f_send.at[kind, s], recv_sem.at[ZS + s], queue, sib
-                )
-                copy.start()
-                forwards.append(copy)
-        for buf, recv_sem in ((v_buf, v_recv), (k_buf, k_recv)):
-            for s in range(ZS):
-                arrived(buf.at[1, s], recv_sem.at[ZS + s])
-        keys = k_buf[...].reshape(2 * ZS * ROWS, DH)
-        vals = v_buf[...].reshape(2 * ZS * ROWS, DH)
+        order = (z, z + 1 - 2 * (z % 2), (z + 2) % ZS, ZS - 1 - z)
+        for s in range(ZS):
+            arrived(v_buf.at[s], v_recv.at[s])
+        pass_values = remote(v_buf, v_sib, f_send.at[ZS], vs_recv, queue, sib)
+        pass_values.start()
+        forwards = [pass_values]
+        for s in order:
+            arrived(kq_buf.at[s], kq_recv.at[s])
+            copy = remote(kq_buf.at[s, 1], k_sib.at[s], f_send.at[s], ks_recv.at[s], queue, sib)
+            copy.start()
+            forwards.append(copy)
+        arrived(v_sib, vs_recv)
+        for s in range(ZS):
+            arrived(k_sib.at[s], ks_recv.at[s])
+        keys = jnp.concatenate(
+            [kq_buf[s, 1] for s in range(ZS)] + [k_sib[s] for s in range(ZS)], axis=0
+        )
+        vals = jnp.concatenate(
+            [v_buf[s] for s in range(ZS)] + [v_sib[s] for s in range(ZS)], axis=0
+        )
         column = lax.broadcasted_iota(jnp.int32, (1, 2 * ZS * ROWS), 1)
         frame = jnp.zeros_like(column)
         for t in range(1, 2 * ZS):
             frame += jnp.where(column >= t * ROWS, 1 if t != ZS else 1 - ZS, 0)
         key_pos = frame - offset
         key_pos = jnp.where(key_pos < 0, key_pos + ZS, key_pos)
-        order = (z, z + 1 - 2 * (z % 2), (z + 2) % ZS, ZS - 1 - z)
 
         def score_into(i):
-            arrived(q_buf.at[order[i]], q_recv.at[order[i]])
             s_buf[i % 2] = lax.dot_general(
-                q_buf[order[i]], keys, (((1,), (1,)), ((), ())), preferred_element_type=jnp.float32
+                kq_buf[order[i], 0], keys, (((1,), (1,)), ((), ())), preferred_element_type=jnp.float32
             )
 
         outs = []
@@ -357,18 +352,16 @@
             p_send.at[kind, rows], rs_buf.at[kind, rows], rs_send.at[kind, p], rs_recv.at[kind, p], q_id, h_id
         )
 
-    send_a, send_b, send_c = [], [], []
+    send_c = []
     p_send[0] = out_block(3).astype(jnp.bfloat16)
-    for p in range(PIECES):
-        send_a.append(rs_copy(0, p, queue, sib))
-        send_a[p].start()
+    send_a = remote(p_send.at[0], rs_buf.at[0], rs_send.at[0, 0], rs_recv.at[0, 0], queue, sib)
+    send_a.start()
     ahead = out_block(2)
     p_send[1] = out_block(1).astype(jnp.bfloat16)
-    for p in range(PIECES):
-        send_b.append(rs_copy(1, p, queue, sib))
-        send_b[p].start()
+    send_b = remote(p_send.at[1], rs_buf.at[1], rs_send.at[1, 0], rs_recv.at[1, 0], queue, sib)
+    send_b.start()
+    arrived(rs_buf.at[0], rs_recv.at[0, 0])
     for p, rows in enumerate(pieces):
-        arrived(rs_buf.at[0, rows], rs_recv.at[0, p])
         mine = ahead[p * PIECE:(p + 1) * PIECE]
         p_send[2, rows] = (mine + rs_buf[0, rows].astype(jnp.float32)).astype(jnp.bfloat16)
         send_c.append(rs_copy(2, p, queue, xnb))
@@ -376,14 +369,13 @@
     proj = out_block(0)
     gate = mod_v[2, pl.ds(noise_ref[position_of((z + 1) % ZS)], 1), columns(0)]
     arrived(lat_next, mv_recv)
-    for p, rows in enumerate(pieces):
-        arrived(rs_buf.at[1, rows], rs_recv.at[1, p])
+    arrived(rs_buf.at[1], rs_recv.at[1, 0])
     proj += rs_buf[1].astype(jnp.float32)
     for p, rows in enumerate(pieces):
         arrived(rs_buf.at[2, rows], rs_recv.at[2, p])
         full = proj[p * PIECE:(p + 1) * PIECE] + rs_buf[2, rows].astype(jnp.float32)
         out_ref[rows] = (lat_next[rows].astype(jnp.float32) + gate * full).astype(jnp.bfloat16)
-    for copy in (*to_x, to_sib, *forward, *stats, *send_a, *send_b, *send_c, lat_move):
+    for copy in (to_x, to_sib, forward, *stats, send_a, send_b, *send_c, lat_move):
         copy.wait_send()
     for mine, far in sends:
         pl.when(jnp.logical_not(mine))(far.wait_send)
@@ -411,10 +403,12 @@
             pltpu.VMEM((ROWS, D), bf16),
             pltpu.VMEM((2, ROWS, WIDTH), f32),
             pltpu.VMEM((4, 8, 256), f32),
-            pltpu.VMEM((3, HEADS_DEV, ROWS, DH), bf16),
+            pltpu.VMEM((HEADS_DEV, 2, ROWS, DH), bf16),
+            pltpu.VMEM((HEADS_DEV, ROWS, DH), bf16),
+            pltpu.VMEM((ZS, 2, ROWS, DH), bf16),
             pltpu.VMEM((ZS, ROWS, DH), bf16),
-            pltpu.VMEM((2, ZS, ROWS, DH), bf16),
-            pltpu.VMEM((2, ZS, ROWS, DH), bf16),
+            pltpu.VMEM((ZS, ROWS, DH), bf16),
+            pltpu.VMEM((ZS, ROWS, DH), bf16),
             pltpu.VMEM((ZS, ROWS, DH), bf16),
             pltpu.VMEM((HEADS_DEV, ROWS, DH), bf16),
             pltpu.VMEM((3, ROWS, WIDTH), bf16),
@@ -422,15 +416,16 @@
             pltpu.VMEM((2, ROWS, 2 * ZS * ROWS), f32),
             pltpu.VMEM((ROWS, WIDTH), bf16),
             dma((7,)),
-            dma((3, PIECES)),
-            dma((4, PIECES)),
+            dma((3,)),
+            dma((4,)),
             dma((4,)),
             dma((4,)),
             dma((3, HEADS_DEV)),
             dma((ZS,)),
-            dma((2 * ZS,)),
-            dma((2 * ZS,)),
-            dma((2, ZS)),
+            dma((ZS,)),
+            dma((ZS,)),
+            dma,
+            dma((ZS + 1,)),
             dma((ZS,)),
             dma((HEADS_DEV,)),
             dma((3, PIECES)),

time: 41.3 us -> 42.5 us (1.029)
  Pallas kernels: 38.7 us -> 40 us
    pallas_call x1, Pallas kernels: 38.7 us -> 40 us  [local_fused(): pl.pallas_call(block_kernel, out_shape=jax.ShapeDtypeStruct((ROWS, WIDTH)...]
where the time goes in v6:
time: 42.5 us; the launch traced here: 42.3 us
  Pallas kernels  40 us (94%)
  other arithmetic  1.69 us (4%)
  between operations  0.68 us (2%)
    pallas_call x1, Pallas kernels, local_fused(): pl.pallas_call(block_kernel, out_shape=jax.ShapeDtypeStruct((ROWS, WIDTH)...  40 us
    select_n x1, other arithmetic, local_fused(): return jnp.where(my_slab // 2 == entry_slot, fresh_half, moved)  1.69 us

profile of v6, /device:TPU:0, one launch (start us, length us, event | category | flops | bytes accessed | tf_op | source)
XLA Modules:
  0.0 42.3 jit_solution(14897426349777367372)
XLA Ops:
  0.7 40.0 %shard_map.91 = bf16[192,384]{1,0:T(8,128)(2,1)} custom-call(s32[1]{0:T(128)S(6)} %copy.10.offset_ref, s32[4]{0:T(128)} %noise_hbm.1, bf16[192,384]{1,0:T(8,128)(2,1)} %lat_hbm.1, f32[384]{0:T(512)} %q_gain_hbm.1, f32[384]{0:T(512)} %k_gain_hbm.1, bf16[3,1536,384]{2,1,0:T(8,128)(2,1)} %bitcast.3, bf16[384,1536]{1,0:T(8,128)(2,1)} %wout_hbm.1, ...), custom_call_target="tpu_custom_call" | custom-call | tf_op jit(solution)/shard_map/pallas_call | solution.py:389
  40.6 1.7 %dynamic-slice_select_fusion = bf16[192,384]{1,0:T(8,128)(2,1)} fusion(bf16[192,384]{1,0:T(8,128)(2,1)} %shard_map.91, bf16[384,384]{1,0:T(8,128)(2,1)} %param.10, s32[]{:T(128)S(6)} %select_n.30, pred[]{:T(512)S(6)} %eq.6), kind=kLoop, calls=%fused_computation | loop fusion | flops 73728 | bytes 442373 | tf_op jit(solution)/shard_map/jit(_where)/select_n | solution.py:452

commit v7 on v3

--- a/solution.py
+++ b/solution.py
@@ -117,7 +117,7 @@
 ROWS = 192
 WIDTH = 384
 HEADS_DEV = 3
-PIECES = 2
+PIECES = 3
 VMEM_BYTES = 64 * 1024 * 1024 - 128 * 1024
 PIECE = ROWS // PIECES
 
@@ -146,6 +146,7 @@
     above = queue + 2 - jnp.where(z == ZS - 1, 2 * ZS, 0)
     swap_head = x * 2 + y
     on_diagonal = y == c
+    order = (ZS - 1 - z, (z + 2) % ZS, z + 1 - 2 * (z % 2), z)
 
     def is_self(zt):
         return jnp.logical_and(on_diagonal, zt == z)
@@ -235,16 +236,18 @@
     sends = []
 
     def send_part(part, buf, recv_sem):
-        for j in range(HEADS_DEV):
-            zt = j + c
-            mine = is_self(zt)
-            src = stage.at[part, j]
+        for i, zt in enumerate(order):
+            valid = jnp.logical_and(zt - c >= 0, zt - c < HEADS_DEV)
+            src = stage.at[part, jnp.where(valid, zt - c, 0)]
             dst = buf.at[z] if part == 0 else buf.at[0, z]
-            far = remote(src, dst, qkv_send.at[part, j], recv_sem.at[z], zt * 2 + c, swap_head)
-            near = pltpu.make_async_copy(src, dst, recv_sem.at[z])
-            pl.when(mine)(near.start)
-            pl.when(jnp.logical_not(mine))(far.start)
-            sends.append((mine, far))
+            far = remote(src, dst, qkv_send.at[part, i], recv_sem.at[z], zt * 2 + c, swap_head)
+            away = valid
+            if i == ZS - 1:
+                near = pltpu.make_async_copy(src, dst, recv_sem.at[z])
+                pl.when(jnp.logical_and(valid, on_diagonal))(near.start)
+                away = jnp.logical_and(valid, jnp.logical_not(on_diagonal))
+            pl.when(away)(far.start)
+            sends.append((away, far))
 
     values = jnp.dot(mod_act[...], w_v[2], preferred_element_type=jnp.float32)
     for j in range(HEADS_DEV):
@@ -291,10 +294,10 @@
     def _():
         forwards = []
         for kind, (buf, recv_sem) in enumerate(((v_buf, v_recv), (k_buf, k_recv))):
-            for s in range(ZS):
+            for i, s in enumerate(order):
                 arrived(buf.at[0, s], recv_sem.at[s])
                 copy = remote(
-                    buf.at[0, s], buf.at[1, s], f_send.at[kind, s], recv_sem.at[ZS + s], queue, sib
+                    buf.at[0, s], buf.at[1, s], f_send.at[kind, i], recv_sem.at[ZS + s], queue, sib
                 )
                 copy.start()
                 forwards.append(copy)
@@ -309,8 +312,6 @@
             frame += jnp.where(column >= t * ROWS, 1 if t != ZS else 1 - ZS, 0)
         key_pos = frame - offset
         key_pos = jnp.where(key_pos < 0, key_pos + ZS, key_pos)
-        order = (z, z + 1 - 2 * (z % 2), (z + 2) % ZS, ZS - 1 - z)
-
         def score_into(i):
             arrived(q_buf.at[order[i]], q_recv.at[order[i]])
             s_buf[i % 2] = lax.dot_general(
@@ -385,8 +386,8 @@
         out_ref[rows] = (lat_next[rows].astype(jnp.float32) + gate * full).astype(jnp.bfloat16)
     for copy in (*to_x, to_sib, *forward, *stats, *send_a, *send_b, *send_c, lat_move):
         copy.wait_send()
-    for mine, far in sends:
-        pl.when(jnp.logical_not(mine))(far.wait_send)
+    for away, far in sends:
+        pl.when(away)(far.wait_send)
 
 
 def local_fused(latents, fresh_frame, noise_level, offset, mod_table, w_qkv, w_out, q_gain, k_gain):
@@ -426,7 +427,7 @@
             dma((4, PIECES)),
             dma((4,)),
             dma((4,)),
-            dma((3, HEADS_DEV)),
+            dma((3, ZS)),
             dma((ZS,)),
             dma((2 * ZS,)),
             dma((2 * ZS,)),

time: 41.3 us -> 41.7 us (level)
  no operation moved by 1% of the time
where the time goes in v7:
time: 41.7 us; the launch traced here: 41.5 us
  Pallas kernels  39.1 us (94%)
  other arithmetic  1.69 us (4%)
  between operations  0.68 us (2%)
    pallas_call x1, Pallas kernels, local_fused(): pl.pallas_call(block_kernel, out_shape=jax.ShapeDtypeStruct((ROWS, WIDTH)...  39.1 us
    select_n x1, other arithmetic, local_fused(): return jnp.where(my_slab // 2 == entry_slot, fresh_half, moved)  1.69 us

profile of v7, /device:TPU:0, one launch (start us, length us, event | category | flops | bytes accessed | tf_op | source)
XLA Modules:
  0.0 41.5 jit_solution(81413088998929685)
XLA Ops:
  0.7 39.1 %shard_map.91 = bf16[192,384]{1,0:T(8,128)(2,1)} custom-call(s32[1]{0:T(128)S(6)} %copy.10.offset_ref, s32[4]{0:T(128)} %noise_hbm.1, bf16[192,384]{1,0:T(8,128)(2,1)} %lat_hbm.1, f32[384]{0:T(512)} %q_gain_hbm.1, f32[384]{0:T(512)} %k_gain_hbm.1, bf16[3,1536,384]{2,1,0:T(8,128)(2,1)} %bitcast.3, bf16[384,1536]{1,0:T(8,128)(2,1)} %wout_hbm.1, ...), custom_call_target="tpu_custom_call" | custom-call | tf_op jit(solution)/shard_map/pallas_call | solution.py:398
  39.8 1.7 %dynamic-slice_select_fusion = bf16[192,384]{1,0:T(8,128)(2,1)} fusion(bf16[192,384]{1,0:T(8,128)(2,1)} %shard_map.91, bf16[384,384]{1,0:T(8,128)(2,1)} %param.10, s32[]{:T(128)S(6)} %select_n.30, pred[]{:T(512)S(6)} %eq.6), kind=kLoop, calls=%fused_computation | loop fusion | flops 73728 | bytes 442373 | tf_op jit(solution)/shard_map/jit(_where)/select_n | solution.py:458

commit v8 on v4

--- a/solution.py
+++ b/solution.py
@@ -145,7 +145,6 @@
     below = queue - 2 + jnp.where(z == 0, 2 * ZS, 0)
     above = queue + 2 - jnp.where(z == ZS - 1, 2 * ZS, 0)
     swap_head = x * 2 + y
-    swap_other = (1 - x) * 2 + y
     on_diagonal = y == c
 
     def is_self(zt):
@@ -174,8 +173,7 @@
     greet(above, head)
     for zt in range(ZS):
         pl.when(jnp.logical_not(is_self(zt)))(lambda zt=zt: greet(zt * 2 + c, swap_head))
-        greet(zt * 2 + c, swap_other)
-    pl.semaphore_wait(barrier, 5 + 2 * ZS - jnp.where(on_diagonal, 1, 0))
+    pl.semaphore_wait(barrier, 5 + ZS - jnp.where(on_diagonal, 1, 0))
 
     def remote(src, dst, s_sem, r_sem, q_id, h_id):
         return pltpu.make_async_remote_copy(
@@ -232,7 +230,6 @@
         copy.start()
         weights.append(copy)
 
-    send_weights(3, 0)
     mean = sum(jnp.sum(block(r), axis=1, keepdims=True) for r in range(4)) / D
     square = jnp.zeros((ROWS, 1), jnp.float32)
     for r in range(4):
@@ -298,8 +295,7 @@
             stage[part, j] = (raw[part, :, cols] * rate * gain[:, cols]).astype(jnp.bfloat16)
         send_part(part, buf, recv_sem)
 
-    send_weights(3, 1)
-    for r in (2, 1):
+    for r in (3, 2, 1):
         for part in range(2):
             send_weights(r, part)
 
@@ -354,11 +350,6 @@
                 o_buf.at[i], a_buf.at[0, slot], o_send.at[0, i], o_recv.at[0, slot], zt * 2 + c, swap_head
             )
             near = pltpu.make_async_copy(o_buf.at[i], a_buf.at[0, slot], o_recv.at[0, slot])
-            other = remote(
-                o_buf.at[i], a_buf.at[2, slot], o_send.at[1, i], o_recv.at[2, slot], zt * 2 + c, swap_other
-            )
-            other.start()
-            forwards.append(other)
             pl.when(mine)(near.start)
             pl.when(jnp.logical_not(mine))(far.start)
             outs.append((mine, far))
@@ -368,14 +359,18 @@
             pl.when(jnp.logical_not(mine))(far.wait_send)
 
     shared = []
+
+    def share(r, to, j, target):
+        copy = remote(
+            a_buf.at[r, j], a_buf.at[to, j], a_send.at[to, j], o_recv.at[to, j], queue, target
+        )
+        copy.start()
+        shared.append(copy)
+
     for j in range(HEADS_DEV):
-        for r in (0, 2):
-            arrived(a_buf.at[r, j], o_recv.at[r, j])
-            copy = remote(
-                a_buf.at[r, j], a_buf.at[r + 1, j], a_send.at[r // 2, j], o_recv.at[r + 1, j], queue, sib
-            )
-            copy.start()
-            shared.append(copy)
+        arrived(a_buf.at[0, j], o_recv.at[0, j])
+        share(0, 2, j, xnb)
+        share(0, 1, j, sib)
 
     def out_block(r):
         attn = jnp.concatenate([a_buf[r, j] for j in range(HEADS_DEV)], axis=1)
@@ -383,6 +378,9 @@
         return jnp.dot(attn, own, preferred_element_type=jnp.float32)
 
     proj = out_block(0)
+    for j in range(HEADS_DEV):
+        arrived(a_buf.at[2, j], o_recv.at[2, j])
+        share(2, 3, j, sib)
     for r in (1, 2, 3):
         for part in range(2):
             rows = pl.ds(part * (WIDTH // 2), WIDTH // 2)
@@ -442,9 +440,9 @@
             dma((2 * ZS,)),
             dma((2 * ZS,)),
             dma((2, ZS)),
-            dma((2, ZS)),
+            dma((1, ZS)),
             dma((4, HEADS_DEV)),
-            dma((2, HEADS_DEV)),
+            dma((4, HEADS_DEV)),
             dma((4, 2)),
             dma((4, 2)),
             dma,

time: 41.7 us -> 40 us (0.959)
  Pallas kernels: 39.3 us -> 37.5 us
    pallas_call x1, Pallas kernels: 39.3 us -> 37.5 us  [local_fused(): pl.pallas_call(block_kernel, out_shape=jax.ShapeDtypeStruct((ROWS, WIDTH)...]
where the time goes in v8:
time: 40 us; the launch traced here: 39.8 us
  Pallas kernels  37.5 us (94%)
  other arithmetic  1.69 us (4%)
  between operations  0.68 us (2%)
    pallas_call x1, Pallas kernels, local_fused(): pl.pallas_call(block_kernel, out_shape=jax.ShapeDtypeStruct((ROWS, WIDTH)...  37.5 us
    select_n x1, other arithmetic, local_fused(): return jnp.where(my_slab // 2 == entry_slot, fresh_half, moved)  1.69 us

profile of v8, /device:TPU:0, one launch (start us, length us, event | category | flops | bytes accessed | tf_op | source)
XLA Modules:
  0.0 39.8 jit_solution(7998685876869031205)
XLA Ops:
  0.7 37.5 %shard_map.91 = bf16[192,384]{1,0:T(8,128)(2,1)} custom-call(s32[1]{0:T(128)S(6)} %copy.10.offset_ref, s32[4]{0:T(128)} %noise_hbm.1, bf16[192,384]{1,0:T(8,128)(2,1)} %lat_hbm.1, f32[384]{0:T(512)} %q_gain_hbm.1, f32[384]{0:T(512)} %k_gain_hbm.1, bf16[3,1536,384]{2,1,0:T(8,128)(2,1)} %bitcast.3, bf16[384,1536]{1,0:T(8,128)(2,1)} %wout_hbm.1, ...), custom_call_target="tpu_custom_call" | custom-call | tf_op jit(solution)/shard_map/pallas_call | solution.py:407
  38.1 1.7 %dynamic-slice_select_fusion = bf16[192,384]{1,0:T(8,128)(2,1)} fusion(bf16[192,384]{1,0:T(8,128)(2,1)} %shard_map.91, bf16[384,384]{1,0:T(8,128)(2,1)} %param.10, s32[]{:T(128)S(6)} %select_n.30, pred[]{:T(512)S(6)} %eq.6), kind=kLoop, calls=%fused_computation | loop fusion | flops 73728 | bytes 442373 | tf_op jit(solution)/shard_map/jit(_where)/select_n | solution.py:467
